TPU v7x, 32 devices: a whole 2x2x4 slice. The times are simulated.
32 devices in a mesh: group: 2 (over x), expert: 8 (over z, y), dp: 2 (over core).
Axes of the slice: x: 2, y: 2, z: 4, core: 2. Of those that a mesh axis runs over, the one named last changes fastest.
Arguments:
- tokens: bfloat16 [8192, 1024], P(('group', 'expert', 'dp')), parts along dimension 0, may hold values from -6 to 6
- routes: int32 [8192, 2], P(('group', 'expert', 'dp')), parts along dimension 0, may hold values from 0 to 63, all different within a row; in each aligned block of 256 rows (0 to 255, 256 to 511, ...) at most 16 rows name the same one
- gate_values: float32 [8192, 2], P(('group', 'expert', 'dp')), parts along dimension 0, may hold values from 0.1 to 1
- up_weight: bfloat16 [64, 1024, 1024], P('expert'), may hold values from -0.1875 to 0.1875
- down_weight: bfloat16 [64, 1024, 1024], P('expert'), may hold values from -0.1875 to 0.1875
- grad_out: bfloat16 [8192, 1024], P(('group', 'expert', 'dp')), parts along dimension 0, may hold values from -6 to 6
Outputs:
- grad_tokens: bfloat16 [8192, 1024], P(('group', 'expert', 'dp')), parts along dimension 0
- grad_gates: float32 [8192, 2], P(('group', 'expert', 'dp')), parts along dimension 0
- grad_up: bfloat16 [128, 1024, 1024], P(('group', 'expert'), 'dp'), parts along dimension 0
- grad_down: bfloat16 [128, 1024, 1024], P(('group', 'expert'), 'dp'), parts along dimension 0
There are 2 independent parts, one for each index of `group`. A program takes and returns all parts, laid end to end along the dimension named above; an argument that names none is the same for every part. Nothing has to cross between parts.
Inputs may be any that keep to these rules, and one draw needn't show every extreme that they name: `routes`: each token names two different experts. Among the 256 tokens of one device no expert is named more than 16 times, and in every draw some expert is named exactly 16 times by the tokens of some device.
All inputs are finite; a program needn't handle non-finite values.
Results may differ from a plain program's by a relative error of at most 0.0065.
Values may be sent and summed in bfloat16 or wider, within the bound.
No kernel may reach another device: no remote copies, remote signals or barrier semaphores. Data moves between devices by JAX's collectives and lax.ppermute only.
A program may use at most 192 MiB of HBM per device.

v0:
```python
import functools

import jax
import jax.numpy as jnp
from jax import lax
from jax.experimental import pallas as pl
from jax.experimental.pallas import tpu as pltpu
from jax.sharding import PartitionSpec as P

EXPERTS = 64
CAP = 16
BF = jnp.bfloat16
F32 = jnp.float32
NT = (((1,), (1,)), ((), ()))
NN = (((1,), (0,)), ((), ()))
TN = (((0,), (0,)), ((), ()))


def dot(a, b, dims, precision=None):
    return lax.dot_general(a, b, dims, preferred_element_type=F32, precision=precision)


COST = pl.CostEstimate(flops=1 << 20, bytes_accessed=1 << 20, transcendentals=0)


def params(mebibytes=14):
    return pltpu.CompilerParams(vmem_limit_bytes=mebibytes * 1024 * 1024)


def targets(routes):
    tokens = routes.shape[1]
    first, second = routes[0:1, :], routes[1:2, :]
    experts = lax.broadcasted_iota(jnp.int32, (EXPERTS, tokens), 0)
    one = (experts == first).astype(F32)
    two = (experts == second).astype(F32)
    earlier = lax.broadcasted_iota(jnp.int32, (tokens, tokens), 0) < lax.broadcasted_iota(
        jnp.int32, (tokens, tokens), 1
    )
    before = dot((one + two).astype(BF), earlier.astype(F32).astype(BF), NN)
    rank_one = jnp.sum(one * before, axis=0, keepdims=True).astype(jnp.int32)
    rank_two = jnp.sum(two * (before + one), axis=0, keepdims=True).astype(jnp.int32)
    return first * CAP + rank_one, second * CAP + rank_two


def thirds(value):
    high = value.astype(BF)
    rest = value - high.astype(F32)
    mid = rest.astype(BF)
    return [high, mid, (rest - mid.astype(F32)).astype(BF)]


def added(rows):
    rows = rows.astype(F32)
    return rows[0:1, :] + rows[1:2, :] + rows[2:3, :]


def prepare_kernel(routes_ref, gates_ref, g_hbm, out_ref, sem):
    tokens, width = g_hbm.shape
    copy = pltpu.make_async_copy(g_hbm, out_ref.at[0:tokens], sem)
    copy.start()
    routes = routes_ref[...].astype(F32).astype(BF)
    gates = gates_ref[...]
    rows = [routes, *thirds(gates[0:1, :]), *thirds(gates[1:2, :]), jnp.zeros((CAP - 8, tokens), BF)]
    out_ref[tokens:, 0:tokens] = jnp.concatenate(rows, axis=0)
    out_ref[tokens:, tokens:] = jnp.zeros((CAP, width - tokens), BF)
    copy.wait()


def prepare(routes, gates, g):
    tokens, width = g.shape
    return pl.pallas_call(
        prepare_kernel,
        out_shape=jax.ShapeDtypeStruct((tokens + CAP, width), BF),
        in_specs=[pl.BlockSpec(memory_space=pltpu.VMEM)] * 2 + [pl.BlockSpec(memory_space=pl.ANY)],
        out_specs=pl.BlockSpec(memory_space=pltpu.VMEM),
        scratch_shapes=[pltpu.SemaphoreType.DMA],
        compiler_params=params(),
        cost_estimate=COST,
        name="prepare",
    )(routes, gates, g)


def facts_of(g_ref, tokens):
    facts = g_ref[tokens : tokens + 8, 0:tokens]
    return targets(facts[0:2, :].astype(F32).astype(jnp.int32)), (added(facts[2:5, :]), added(facts[5:8, :]))


def select_slots(targets_of, gates, base, slots):
    rows = lax.broadcasted_iota(jnp.int32, (slots, targets_of[0].shape[1]), 0) + base
    is_one, is_two = rows == targets_of[0], rows == targets_of[1]
    gate = jnp.where(is_one, gates[0], 0.0) + jnp.where(is_two, gates[1], 0.0)
    return jnp.where(is_one | is_two, 1.0, 0.0).astype(BF), jnp.sum(gate, axis=1, keepdims=True)


def whole(*shape):
    return pl.BlockSpec(shape, lambda j: (0,) * len(shape), pipeline_mode=pl.Buffered(1))


def by_expert(*shape):
    return pl.BlockSpec(shape, lambda j: (j,) + (0,) * (len(shape) - 1))


def d_kernel(peers, me_ref, g_ref, select_ref, facts_ref, *d_refs):
    slots, tokens = select_ref.shape[1:]
    tgt, gates = facts_of(g_ref, tokens)
    for m in range(peers):
        select, gate = select_slots(tgt, gates, (me_ref[0] ^ m) * slots, slots)
        select_ref[m] = select
        d_refs[m][...] = (gate * dot(select, g_ref[0:tokens], NN)).astype(BF)
    facts_ref[0:2] = jnp.concatenate(tgt, axis=0).astype(F32)
    facts_ref[2:4] = jnp.concatenate(gates, axis=0)
    facts_ref[4:8] = jnp.zeros((4, tokens), F32)


SCALARS = pl.BlockSpec(memory_space=pltpu.SMEM)
VECTORS = pl.BlockSpec(memory_space=pltpu.VMEM)


def d_pass(name, me, g, peers, slots):
    tokens, width = g.shape[0] - CAP, g.shape[1]
    out = pl.pallas_call(
        functools.partial(d_kernel, peers),
        out_shape=[jax.ShapeDtypeStruct((peers, slots, tokens), BF), jax.ShapeDtypeStruct((8, tokens), F32)]
        + [jax.ShapeDtypeStruct((slots, width), BF)] * peers,
        in_specs=[SCALARS, VECTORS],
        out_specs=[VECTORS] * (2 + peers),
        compiler_params=params(),
        cost_estimate=COST,
        name=name,
    )(me, g)
    return out[0], out[1], list(out[2:])


def x_kernel(peers, near_ref, x_near_ref, far_ref, x_far_ref, *out_refs):
    slots = near_ref.shape[1]
    for m in range(peers):
        out_refs[m][0:slots] = dot(near_ref[m], x_near_ref[...], NN).astype(BF)
        out_refs[m][slots:] = dot(far_ref[m], x_far_ref[...], NN).astype(BF)


def x_pass(select_near, x_near, select_far, x_far):
    peers, slots, _ = select_near.shape
    return list(
        pl.pallas_call(
            functools.partial(x_kernel, peers),
            out_shape=[jax.ShapeDtypeStruct((2 * slots, x_near.shape[1]), BF)] * peers,
            in_specs=[VECTORS] * 4,
            out_specs=[VECTORS] * peers,
            compiler_params=params(),
            cost_estimate=COST,
            name="x_rows",
        )(select_near, x_near, select_far, x_far)
    )


IN_HBM = pl.BlockSpec(memory_space=pltpu.HBM)


def in_hbm(value):
    return pltpu.with_memory_space_constraint(value, pltpu.HBM)


def fetch(weight_hbm, weight_ref, sem):
    copies = [
        pltpu.make_async_copy(weight_hbm.at[j], weight_ref.at[j], sem.at[j]) for j in range(weight_hbm.shape[0])
    ]
    for copy in copies:
        copy.start()
    return copies


def joined(parts):
    return jnp.concatenate(parts, axis=0)


def of_expert(j, first=0):
    return slice(first + j * CAP, first + (j + 1) * CAP)


def expert_rows(j, refs, first=0):
    return [ref[first + j * CAP : first + (j + 1) * CAP] for ref in refs]


def down_kernel(peers, weight_hbm, *refs):
    d_refs, (h_ref, d_ref, weight_ref, sem) = refs[: 2 * peers], refs[2 * peers :]
    for j, copy in enumerate(fetch(weight_hbm, weight_ref, sem)):
        rows = joined(expert_rows(j, d_refs))
        d_ref[j] = rows
        copy.wait()
        h_ref[j] = dot(rows, weight_ref[j], NT)


def down_pass(weight, near_d, far_d):
    experts, hidden, width = weight.shape
    peers = len(near_d)
    rows = 2 * peers * CAP
    return pl.pallas_call(
        functools.partial(down_kernel, peers),
        out_shape=[
            jax.ShapeDtypeStruct((experts, rows, hidden), F32),
            jax.ShapeDtypeStruct((experts, rows, width), BF),
        ],
        in_specs=[IN_HBM] + [VECTORS] * (2 * peers),
        out_specs=[VECTORS] * 2,
        scratch_shapes=[pltpu.VMEM(weight.shape, BF), pltpu.SemaphoreType.DMA((experts,))],
        compiler_params=params(24),
        cost_estimate=COST,
        name="down_pass",
    )(in_hbm(weight), *near_d, *far_d)


def up_kernel(peers, core_ref, weight_hbm, h_ref, *refs):
    groups, refs = [refs[i * peers : (i + 1) * peers] for i in range(4)], refs[4 * peers :]
    x_refs, near_gx_refs, one_refs, two_refs = groups
    pack_hbm, mine_hbm, weight_ref, part_ref, pack_ref, mine_ref, in_sem, out_sem = refs
    experts = weight_ref.shape[0]
    width, cols = x_refs[0].shape[1], one_refs[0].shape[1]
    slots, half = experts * CAP, mine_ref.shape[2] // 2
    core = core_ref[0]

    def store(j):
        return (
            pltpu.make_async_copy(pack_ref.at[j], pack_hbm.at[j], out_sem.at[j, 0]),
            pltpu.make_async_copy(mine_ref.at[j], mine_hbm.at[j], out_sem.at[j, 1]),
        )

    copies = fetch(weight_hbm, weight_ref, in_sem)

    def before(j):
        copies[j].wait()
        x = joined(expert_rows(j, x_refs) + expert_rows(j, x_refs, slots))
        pack_ref[j, :, 0:width] = x
        return dot(x, weight_ref[j], NT)

    following = before(0)
    for j in range(experts):
        at = of_expert(j)
        pre, h = following, h_ref[j]
        following = before(j + 1) if j + 1 < experts else None
        sig = 1.0 / (1.0 + jnp.exp(-pre))
        active = (pre * sig).astype(BF)
        grad_pre = (h * sig * (1.0 + pre * (1.0 - sig))).astype(BF)
        gx = dot(grad_pre, weight_ref[j], NN).astype(BF)
        prod = active.astype(F32) * h
        part = prod[:, 0:128]
        for i in range(1, prod.shape[1] // 128):
            part = part + prod[:, i * 128 : (i + 1) * 128]
        for m in range(peers):
            near, far = of_expert(m), of_expert(peers + m)
            part_ref[m, at], part_ref[peers + m, at] = part[near], part[far]
            near_gx_refs[m][at] = gx[near]
            one_refs[m][at] = gx[far, 0:cols]
            two_refs[m][at] = gx[far, cols:]
        for i, value in enumerate((active, grad_pre)):
            low, high = value[:, 0:half], value[:, half:]
            to = i * half
            mine_ref[j, :, to : to + half] = jnp.where(core == 0, low, high)
            pack_ref[j, :, width + to : width + to + half] = jnp.where(core == 0, high, low)
        for out in store(j):
            out.start()
    for m, ref in enumerate((*near_gx_refs, *one_refs)):
        total = jnp.sum(part_ref[m].T, axis=0, keepdims=True)
        ref[slots : slots + CAP, 0:slots] = joined([*thirds(total), jnp.zeros((CAP - 3, slots), BF)])
        ref[slots : slots + CAP, slots:] = jnp.zeros((CAP, ref.shape[1] - slots), BF)
    for j in range(experts):
        for out in store(j):
            out.wait()


def up_pass(core, weight, h, x):
    experts, hidden, width = weight.shape
    peers = len(x)
    count, slots, cols = 2 * peers * CAP, experts * CAP, width // 2
    pack = (experts, count, width + hidden)
    mine = (experts, count, hidden)
    shapes = [(slots + CAP, width)] * peers + [(slots + CAP, cols)] * peers + [(slots, cols)] * peers
    out = pl.pallas_call(
        functools.partial(up_kernel, peers),
        out_shape=[jax.ShapeDtypeStruct(shape, BF) for shape in (*shapes, pack, mine)],
        in_specs=[SCALARS, IN_HBM] + [VECTORS] * (1 + peers),
        out_specs=[VECTORS] * (3 * peers) + [pl.BlockSpec(memory_space=pl.ANY)] * 2,
        scratch_shapes=[
            pltpu.VMEM(weight.shape, BF),
            pltpu.VMEM((2 * peers, slots, 128), F32),
            pltpu.VMEM(pack, BF),
            pltpu.VMEM(mine, BF),
            pltpu.SemaphoreType.DMA((experts,)),
            pltpu.SemaphoreType.DMA((experts, 2)),
        ],
        compiler_params=params(28),
        cost_estimate=COST,
        name="up_pass",
    )(core, in_hbm(weight), h, *x)
    return *(list(out[i * peers : (i + 1) * peers]) for i in range(3)), out[-2], out[-1]


def weight_kernel(mine_ref, pack_ref, other_ref, d_ref, d_other_ref, up_ref, down_ref):
    half, width = up_ref.shape[1:]
    active = joined([mine_ref[0, :, 0:half], other_ref[0, :, width : width + half]])
    grad_pre = joined([mine_ref[0, :, half:], other_ref[0, :, width + half :]])
    up_ref[0] = dot(grad_pre, joined([pack_ref[0], other_ref[0, :, 0:width]]), TN).astype(BF)
    down_ref[0] = dot(active, joined([d_ref[0], d_other_ref[0]]), TN).astype(BF)


def weight_pass(mine, pack, other, d, d_other):
    experts, rows, width = d.shape
    hidden = mine.shape[2]
    return pl.pallas_call(
        weight_kernel,
        grid=(experts,),
        out_shape=[jax.ShapeDtypeStruct((experts, hidden // 2, width), BF)] * 2,
        in_specs=[by_expert(1, rows, n) for n in (hidden, width, width + hidden, width, width)],
        out_specs=[by_expert(1, hidden // 2, width)] * 2,
        compiler_params=params(),
        cost_estimate=COST,
        name="weight_pass",
    )(mine, pack, other, d, d_other)


def relay_kernel(peers, select_ref, *refs):
    out_ref = refs[peers]
    slots, tokens = select_ref.shape[1:]
    total = None
    for m in range(peers):
        term = dot(select_ref[m], refs[m][0:slots], TN)
        total = term if total is None else total + term
    out_ref[0:tokens] = total.astype(BF)
    if refs[0].shape[0] > slots:
        for m in range(peers):
            out_ref[tokens + m * CAP : tokens + (m + 1) * CAP] = refs[m][slots:]


def relay_pass(select, rows):
    peers, slots, tokens = select.shape
    width = rows[0].shape[1]
    out_rows = tokens + peers * (rows[0].shape[0] - slots)
    return pl.pallas_call(
        functools.partial(relay_kernel, peers),
        out_shape=jax.ShapeDtypeStruct((out_rows, width), BF),
        in_specs=[VECTORS] * (1 + peers),
        out_specs=VECTORS,
        compiler_params=params(),
        cost_estimate=COST,
        name="relay_sum",
    )(select, *rows)


def last_kernel(me_ref, facts_ref, select_ref, one_ref, two_ref, *refs):
    near_refs, (out_ref, gates_ref) = refs[:-2], refs[-2:]
    peers, slots, tokens = select_ref.shape
    cols = one_ref.shape[1]
    me = me_ref[0]
    tgt = facts_ref[0:1, :].astype(jnp.int32), facts_ref[1:2, :].astype(jnp.int32)
    total = None
    values = [jnp.zeros((1, tokens), F32)] * 2
    for m in range(peers):
        term = dot(select_ref[m], near_refs[m][0:slots], TN)
        total = term if total is None else total + term
        far = one_ref[tokens + m * CAP : tokens + (m + 1) * CAP, 0:slots]
        near = near_refs[m][slots : slots + CAP, 0:slots]
        for chip, tail in ((me ^ m, near), (me ^ (peers + m), far)):
            column = added(tail).T
            at = lax.broadcasted_iota(jnp.int32, (slots, tokens), 0) + chip * slots
            for k in range(2):
                hit = jnp.where(at == tgt[k], column, 0.0)
                values[k] = values[k] + jnp.sum(hit, axis=0, keepdims=True)
    gates_ref[0:1] = values[0] / facts_ref[2:3, :]
    gates_ref[1:2] = values[1] / facts_ref[3:4, :]
    total = total.astype(BF).astype(F32)
    out_ref[:, 0:cols] = (total[:, 0:cols] + one_ref[0:tokens].astype(F32)).astype(BF)
    out_ref[:, cols:] = (total[:, cols:] + two_ref[...].astype(F32)).astype(BF)


def last_pass(me, facts, select, near, one, two):
    tokens = select.shape[2]
    width = one.shape[1] + two.shape[1]
    return pl.pallas_call(
        last_kernel,
        out_shape=[jax.ShapeDtypeStruct((tokens, width), BF), jax.ShapeDtypeStruct((2, tokens), F32)],
        in_specs=[SCALARS] + [VECTORS] * (4 + len(near)),
        out_specs=[VECTORS] * 2,
        compiler_params=params(),
        cost_estimate=COST,
        name="last_sum",
    )(me, facts, select, one, two, *near)


def after(value, *others):
    return lax.optimization_barrier((value, *others))[0]


def per_device(tokens, routes, gate_values, up_weight, down_weight, grad_out):
    chips = lax.axis_size("expert")
    half = chips // 2
    slots = up_weight.shape[0] * CAP
    me = lax.axis_index("expert").astype(jnp.int32).reshape(1)
    core = lax.axis_index("dp").astype(jnp.int32).reshape(1)

    def swap(value, m):
        return lax.ppermute(value, "expert", [(i, i ^ m) for i in range(chips)])

    def swap_core(value):
        return lax.ppermute(value, "dp", [(0, 1), (1, 0)])

    def deal(rows):
        return [rows[0]] + [swap(rows[m], m) for m in range(1, half)]

    g_near = prepare(routes.T, gate_values.T, grad_out)
    g_far = swap(g_near, half)
    select, facts, near_d = d_pass("near_d_rows", me, g_near, half, slots)
    near_d = deal(near_d)
    x_far = swap(after(tokens, g_far, near_d), half)

    select_far, _, far_d = d_pass("far_d_rows", me, g_far, half, slots)
    far_d = deal(far_d)
    x = x_pass(select, tokens, select_far, after(x_far, far_d))
    h, d = down_pass(down_weight, near_d, after(far_d, x[0]))
    d_other = swap_core(d)
    gx_near, gx_one, gx_two, pack, mine = up_pass(core, up_weight, h, deal(x))
    gx_one, gx_two = deal(gx_one), deal(gx_two)
    other = swap_core(pack)

    relay_one = relay_pass(select_far, after(gx_one, d_other))
    back_one = swap(relay_one, half)
    relay_two = relay_pass(select_far, after(gx_two, other))
    back_two = swap(relay_two, half)
    gx_near = deal(after(gx_near, relay_two))

    grad_up, grad_down = weight_pass(after(mine, relay_two), pack, other, d, d_other)
    grad_tokens, grad_gates = last_pass(me, after(facts, grad_up), select, gx_near, back_one, back_two)
    return grad_tokens, grad_gates.T, grad_up, grad_down


def solution(mesh):
    placed = (
        P(("group", "expert", "dp"), None),
        P(("group", "expert", "dp"), None),
        P(("group", "expert", "dp"), None),
        P("expert", None, None),
        P("expert", None, None),
        P(("group", "expert", "dp"), None),
    )
    return jax.shard_map(
        per_device,
        mesh=mesh,
        in_specs=placed,
        out_specs=(
            P(("group", "expert", "dp"), None),
            P(("group", "expert", "dp"), None),
            P(("group", "expert"), "dp", None),
            P(("group", "expert"), "dp", None),
        ),
        check_vma=False,
    )
```

profile of v0, /device:TPU:0, one launch (start us, length us, event | category | flops | bytes accessed | tf_op | source)
XLA Modules:
  0.0 146.3 jit_solution(17319885642768340356)
XLA Ops:
  0.6 1.0 copy-done.1
  1.7 0.7 copy-done.14
  2.4 0.7 copy-done.15
  3.1 4.1 %collective-permute-start.3 = (bf16[272,1024]{1,0:T(8,128)(2,1)S(1)}, bf16[272,1024]{1,0:T(8,128)(2,1)S(1)}, u32[]{:S(2)}, u32[]{:S(2)}) collective-permute-start(bf16[272,1024]{1,0:T(8,128)(2,1)S(1)} %prepare.1.g_ref), channel_id=1, source_target_pairs={{0,8},{2,10},{4,12},{6,14},{8,0},{10,2},{12,4},{14,6},{1,9},{3,11}... | collective-permute-start | bytes 1671176 | tf_op jit(solution)/shard_map/ppermute | solution.py:400
  7.2 0.8 near_d_rows.1
  8.0 1.6 %collective-permute-start = (bf16[128,1024]{1,0:T(8,128)(2,1)S(1)}, bf16[128,1024]{1,0:T(8,128)(2,1)S(1)}, u32[]{:S(2)}, u32[]{:S(2)}) collective-permute-start(bf16[128,1024]{1,0:T(8,128)(2,1)S(1)} %get-tuple-element.61), channel_id=1, source_target_pairs={{0,2},{2,0},{4,6},{6,4},{8,10},{10,8},{12,14},{14,12},{1,3},{3,1},... | collective-permute-start | bytes 786440 | tf_op jit(solution)/shard_map/ppermute | solution.py:400
  9.6 1.6 %collective-permute-start.1 = (bf16[128,1024]{1,0:T(8,128)(2,1)S(1)}, bf16[128,1024]{1,0:T(8,128)(2,1)S(1)}, u32[]{:S(2)}, u32[]{:S(2)}) collective-permute-start(bf16[128,1024]{1,0:T(8,128)(2,1)S(1)} %get-tuple-element.62), channel_id=1, source_target_pairs={{0,4},{2,6},{4,0},{6,2},{8,12},{10,14},{12,8},{14,10},{1,5},{3,7},... | collective-permute-start | bytes 786440 | tf_op jit(solution)/shard_map/ppermute | solution.py:400
  11.5 4.8 %collective-permute-done.refs_1_ = bf16[128,1024]{1,0:T(8,128)(2,1)S(1)} collective-permute-done((bf16[128,1024]{1,0:T(8,128)(2,1)S(1)}, bf16[128,1024]{1,0:T(8,128)(2,1)S(1)}, u32[]{:S(2)}, u32[]{:S(2)}) %collective-permute-start) | collective-permute-done | bytes 262176 | tf_op jit(solution)/shard_map/ppermute | solution.py:400
  16.4 9.5 %collective-permute-done.1.refs_2_ = bf16[128,1024]{1,0:T(8,128)(2,1)S(1)} collective-permute-done((bf16[128,1024]{1,0:T(8,128)(2,1)S(1)}, bf16[128,1024]{1,0:T(8,128)(2,1)S(1)}, u32[]{:S(2)}, u32[]{:S(2)}) %collective-permute-start.1) | collective-permute-done | bytes 262176 | tf_op jit(solution)/shard_map/ppermute | solution.py:400
  25.9 7.5 %collective-permute-done.2.refs_3_ = bf16[128,1024]{1,0:T(8,128)(2,1)S(1)} collective-permute-done((bf16[128,1024]{1,0:T(8,128)(2,1)S(1)}, bf16[128,1024]{1,0:T(8,128)(2,1)S(1)}, u32[]{:S(2)}, u32[]{:S(2)}) %collective-permute-start.2) | collective-permute-done | bytes 262176 | tf_op jit(solution)/shard_map/ppermute | solution.py:400
  34.0 1.3 far_d_rows.1
  35.3 0.9 collective-permute-start.4
  36.2 3.0 %collective-permute-start.5 = (bf16[128,1024]{1,0:T(8,128)(2,1)S(1)}, bf16[128,1024]{1,0:T(8,128)(2,1)S(1)}, u32[]{:S(2)}, u32[]{:S(2)}) collective-permute-start(bf16[128,1024]{1,0:T(8,128)(2,1)S(1)} %get-tuple-element.66), channel_id=1, source_target_pairs={{0,4},{2,6},{4,0},{6,2},{8,12},{10,14},{12,8},{14,10},{1,5},{3,7},... | collective-permute-start | bytes 786440 | tf_op jit(solution)/shard_map/ppermute | solution.py:400
  39.2 2.8 %collective-permute-done.4.refs_5_ = bf16[128,1024]{1,0:T(8,128)(2,1)S(1)} collective-permute-done((bf16[128,1024]{1,0:T(8,128)(2,1)S(1)}, bf16[128,1024]{1,0:T(8,128)(2,1)S(1)}, u32[]{:S(2)}, u32[]{:S(2)}) %collective-permute-start.4) | collective-permute-done | bytes 262176 | tf_op jit(solution)/shard_map/ppermute | solution.py:400
  41.9 10.3 %collective-permute-done.5.refs_6_ = bf16[128,1024]{1,0:T(8,128)(2,1)S(1)} collective-permute-done((bf16[128,1024]{1,0:T(8,128)(2,1)S(1)}, bf16[128,1024]{1,0:T(8,128)(2,1)S(1)}, u32[]{:S(2)}, u32[]{:S(2)}) %collective-permute-start.5) | collective-permute-done | bytes 262176 | tf_op jit(solution)/shard_map/ppermute | solution.py:400
  52.2 0.7 copy-done.10
  52.9 6.6 %collective-permute-done.6.refs_7_ = bf16[128,1024]{1,0:T(8,128)(2,1)S(1)} collective-permute-done((bf16[128,1024]{1,0:T(8,128)(2,1)S(1)}, bf16[128,1024]{1,0:T(8,128)(2,1)S(1)}, u32[]{:S(2)}, u32[]{:S(2)}) %collective-permute-start.6) | collective-permute-done | bytes 262176 | tf_op jit(solution)/shard_map/ppermute | solution.py:400
  59.5 0.7 copy-done.12
  60.2 1.0 copy-done
  61.3 1.6 %x_rows.1 = (bf16[256,1024]{1,0:T(8,128)(2,1)S(1)}, bf16[256,1024]{1,0:T(8,128)(2,1)}, bf16[256,1024]{1,0:T(8,128)(2,1)}, bf16[256,1024]{1,0:T(8,128)(2,1)}) custom-call(bf16[4,128,256]{2,1,0:T(8,128)(2,1)S(1)} %get-tuple-element.68.near_ref.select_ref, bf16[256,1024]{1,0:T(8,128)(2,1)S(1)} %copy-done, ...), custom_call_target="tpu_custom_call" | custom-call | flops 1048576 | bytes 1048576 | tf_op jit(solution)/shard_map/x_rows/pallas_call | solution.py:144
  62.9 1.7 %collective-permute-start.8 = (bf16[256,1024]{1,0:T(8,128)(2,1)}, bf16[256,1024]{1,0:T(8,128)(2,1)S(1)}, u32[]{:S(2)}, u32[]{:S(2)}) collective-permute-start(bf16[256,1024]{1,0:T(8,128)(2,1)} %get-tuple-element.78), channel_id=1, source_target_pairs={{0,2},{2,0},{4,6},{6,4},{8,10},{10,8},{12,14},{14,12},{1,3},{3,1},... | collective-permute-start | bytes 1572872 | tf_op jit(solution)/shard_map/ppermute | solution.py:400
  64.6 1.8 %collective-permute-start.10 = (bf16[256,1024]{1,0:T(8,128)(2,1)}, bf16[256,1024]{1,0:T(8,128)(2,1)S(1)}, u32[]{:S(2)}, u32[]{:S(2)}) collective-permute-start(bf16[256,1024]{1,0:T(8,128)(2,1)} %get-tuple-element.80), channel_id=1, source_target_pairs={{0,6},{2,4},{4,2},{6,0},{8,14},{10,12},{12,10},{14,8},{1,7},{3,5},... | collective-permute-start | bytes 1572872 | tf_op jit(solution)/shard_map/ppermute | solution.py:400
  66.4 0.9 copy-done.3
  67.4 0.9 copy-done.5
  68.3 0.9 copy-done.7
  69.3 0.9 copy-done.9
  70.2 0.9 copy-done.11
  71.2 0.9 copy-done.13
  72.1 8.3 %down_pass.1 = (f32[8,128,1024]{2,1,0:T(8,128)S(1)}, bf16[8,128,1024]{2,1,0:T(8,128)(2,1)S(1)}) custom-call(bf16[8,1024,1024]{2,1,0:T(8,128)(2,1)} %weight_hbm.2, bf16[128,1024]{1,0:T(8,128)(2,1)S(1)} %get-tuple-element.60.refs_0_, bf16[128,1024]{1,0:T(8,128)(2,1)S(1)} %collective-permute-done.refs_1_, bf16[128,1024]{1,0:T(8,128)(2,1)S(1)} %copy-done.3, ...), custom_call_target="tpu_custom_call" | custom-call | flops 1048576 | bytes 1048576 | tf_op jit(solution)/shard_map/down_pass/pallas_call | solution.py:197
  80.5 7.7 %collective-permute-done.10.refs_3_ = bf16[256,1024]{1,0:T(8,128)(2,1)S(1)} collective-permute-done((bf16[256,1024]{1,0:T(8,128)(2,1)}, bf16[256,1024]{1,0:T(8,128)(2,1)S(1)}, u32[]{:S(2)}, u32[]{:S(2)}) %collective-permute-start.10) | collective-permute-done | bytes 524320 | tf_op jit(solution)/shard_map/ppermute | solution.py:400
  88.2 13.2 %up_pass.1 = (bf16[144,1024]{1,0:T(8,128)(2,1)S(1)}, bf16[144,1024]{1,0:T(8,128)(2,1)S(1)}, bf16[144,1024]{1,0:T(8,128)(2,1)S(1)}, bf16[144,1024]{1,0:T(8,128)(2...) custom-call(s32[1]{0:T(128)} %bitcast.3.core_ref, ...), custom_call_target="tpu_custom_call" | custom-call | flops 1048576 | bytes 1048576 | tf_op jit(solution)/shard_map/up_pass/pallas_call | solution.py:277
  101.9 1.2 collective-permute-start.16
  103.4 2.0 %collective-permute-start.18 = (bf16[144,512]{1,0:T(8,128)(2,1)S(1)}, bf16[144,512]{1,0:T(8,128)(2,1)S(1)}, u32[]{:S(2)}, u32[]{:S(2)}) collective-permute-start(bf16[144,512]{1,0:T(8,128)(2,1)S(1)} %get-tuple-element.98), channel_id=1, source_target_pairs={{0,6},{2,4},{4,2},{6,0},{8,14},{10,12},{12,10},{14,8},{1,7},{3,5},... | collective-permute-start | bytes 442376 | tf_op jit(solution)/shard_map/ppermute | solution.py:400
  105.4 2.3 %collective-permute-done.16.refs_1_ = bf16[144,512]{1,0:T(8,128)(2,1)S(1)} collective-permute-done((bf16[144,512]{1,0:T(8,128)(2,1)S(1)}, bf16[144,512]{1,0:T(8,128)(2,1)S(1)}, u32[]{:S(2)}, u32[]{:S(2)}) %collective-permute-start.16) | collective-permute-done | bytes 147488 | tf_op jit(solution)/shard_map/ppermute | solution.py:400
  107.8 1.2 collective-permute-start.11
  109.0 0.9 collective-permute-done.17.refs_2_
  110.2 3.1 %collective-permute-done.18.refs_3_ = bf16[144,512]{1,0:T(8,128)(2,1)S(1)} collective-permute-done((bf16[144,512]{1,0:T(8,128)(2,1)S(1)}, bf16[144,512]{1,0:T(8,128)(2,1)S(1)}, u32[]{:S(2)}, u32[]{:S(2)}) %collective-permute-start.18) | collective-permute-done | bytes 147488 | tf_op jit(solution)/shard_map/ppermute | solution.py:400
  113.3 0.9 collective-permute-start.13
  114.7 3.4 %collective-permute-start.19 = (bf16[320,512]{1,0:T(8,128)(2,1)S(1)}, bf16[320,512]{1,0:T(8,128)(2,1)S(1)}, u32[]{:S(2)}, u32[]{:S(2)}) collective-permute-start(bf16[320,512]{1,0:T(8,128)(2,1)S(1)} %relay_sum.3), channel_id=1, source_target_pairs={{0,8},{2,10},{4,12},{6,14},{8,0},{10,2},{12,4},{14,6},{1,9},{3,11}... | collective-permute-start | bytes 983048 | tf_op jit(solution)/shard_map/ppermute | solution.py:400
  118.1 1.4 collective-permute-done.13.refs_3_
  120.0 1.2 collective-permute-start.21
  121.2 1.1 collective-permute-start.22
  122.3 1.2 collective-permute-start.23
  123.5 2.5 %collective-permute-start.20 = (bf16[256,512]{1,0:T(8,128)(2,1)S(1)}, bf16[256,512]{1,0:T(8,128)(2,1)S(1)}, u32[]{:S(2)}, u32[]{:S(2)}) collective-permute-start(bf16[256,512]{1,0:T(8,128)(2,1)S(1)} %relay_sum.2), channel_id=1, source_target_pairs={{0,8},{2,10},{4,12},{6,14},{8,0},{10,2},{12,4},{14,6},{1,9},{3,11}... | collective-permute-start | bytes 786440 | tf_op jit(solution)/shard_map/ppermute | solution.py:400
  126.0 7.9 %weight_pass.1 = (bf16[8,512,1024]{2,1,0:T(8,128)(2,1)}, bf16[8,512,1024]{2,1,0:T(8,128)(2,1)}) custom-call(bf16[8,128,1024]{2,1,0:T(8,128)(2,1)S(1)} %get-tuple-element.91.mine_ref, bf16[8,128,2048]{2,1,0:T(8,128)(2,1)S(1)} %get-tuple-element.86.pack_ref, bf16[8,128,2048]{2,1,0:T(8,128)(2,1)S(1)} %collective-permute-done.14.other_ref, ...), custom_call_target="tpu_custom_call" | custom-call | flops 1048576 | bytes 1048576 | tf_op jit(solution)/shard_map/weight_pass/pallas_call | solution.py:308
  134.0 8.0 %collective-permute-done.20.two_ref = bf16[256,512]{1,0:T(8,128)(2,1)S(1)} collective-permute-done((bf16[256,512]{1,0:T(8,128)(2,1)S(1)}, bf16[256,512]{1,0:T(8,128)(2,1)S(1)}, u32[]{:S(2)}, u32[]{:S(2)}) %collective-permute-start.20) | collective-permute-done | bytes 262176 | tf_op jit(solution)/shard_map/ppermute | solution.py:400
  142.0 2.5 %collective-permute-done.23.refs_3_ = bf16[144,1024]{1,0:T(8,128)(2,1)S(1)} collective-permute-done((bf16[144,1024]{1,0:T(8,128)(2,1)S(1)}, bf16[144,1024]{1,0:T(8,128)(2,1)S(1)}, u32[]{:S(2)}, u32[]{:S(2)}) %collective-permute-start.23) | collective-permute-done | bytes 294944 | tf_op jit(solution)/shard_map/ppermute | solution.py:400
  144.6 1.7 %last_sum.1 = (bf16[256,1024]{1,0:T(8,128)(2,1)}, f32[2,256]{1,0:T(2,128)}) custom-call(s32[1]{0:T(128)} %bitcast.me_ref, f32[8,256]{1,0:T(8,128)S(1)} %get-tuple-element.94.facts_ref, bf16[4,128,256]{2,1,0:T(8,128)(2,1)S(1)} %get-tuple-element.68.near_ref.select_ref, bf16[320,512]{1,0:T(8,128)(2,1)S(1)} %collective-permute-done.19.one_ref, ...), custom_call_target="tpu_custom_call" | custom-call | flops 1048576 | bytes 1048576 | tf_op jit(solution)/shard_map/last_sum/pallas_call | solution.py:377
  (42 shorter events, 3.1 us)
Async XLA Ops:
  0.6 1.0 copy-start.1
  1.7 0.7 copy-start.14
  2.4 0.7 copy-start.15
  3.1 30.3 %collective-permute-start.3 = (bf16[272,1024]{1,0:T(8,128)(2,1)S(1)}, bf16[272,1024]{1,0:T(8,128)(2,1)S(1)}, u32[]{:S(2)}, u32[]{:S(2)}) collective-permute-start(bf16[272,1024]{1,0:T(8,128)(2,1)S(1)} %prepare.1.g_ref), channel_id=1, source_target_pairs={{0,8},{2,10},{4,12},{6,14},{8,0},{10,2},{12,4},{14,6},{1,9},{3,11}... | collective-permute-start | bytes 1671176 | tf_op jit(solution)/shard_map/ppermute | solution.py:400
  8.0 8.4 %collective-permute-start = (bf16[128,1024]{1,0:T(8,128)(2,1)S(1)}, bf16[128,1024]{1,0:T(8,128)(2,1)S(1)}, u32[]{:S(2)}, u32[]{:S(2)}) collective-permute-start(bf16[128,1024]{1,0:T(8,128)(2,1)S(1)} %get-tuple-element.61), channel_id=1, source_target_pairs={{0,2},{2,0},{4,6},{6,4},{8,10},{10,8},{12,14},{14,12},{1,3},{3,1},... | collective-permute-start | bytes 786440 | tf_op jit(solution)/shard_map/ppermute | solution.py:400
  9.6 16.4 %collective-permute-start.1 = (bf16[128,1024]{1,0:T(8,128)(2,1)S(1)}, bf16[128,1024]{1,0:T(8,128)(2,1)S(1)}, u32[]{:S(2)}, u32[]{:S(2)}) collective-permute-start(bf16[128,1024]{1,0:T(8,128)(2,1)S(1)} %get-tuple-element.62), channel_id=1, source_target_pairs={{0,4},{2,6},{4,0},{6,2},{8,12},{10,14},{12,8},{14,10},{1,5},{3,7},... | collective-permute-start | bytes 786440 | tf_op jit(solution)/shard_map/ppermute | solution.py:400
  11.1 22.3 %collective-permute-start.2 = (bf16[128,1024]{1,0:T(8,128)(2,1)S(1)}, bf16[128,1024]{1,0:T(8,128)(2,1)S(1)}, u32[]{:S(2)}, u32[]{:S(2)}) collective-permute-start(bf16[128,1024]{1,0:T(8,128)(2,1)S(1)} %get-tuple-element.63), channel_id=1, source_target_pairs={{0,6},{2,4},{4,2},{6,0},{8,14},{10,12},{12,10},{14,8},{1,7},{3,5},... | collective-permute-start | bytes 786440 | tf_op jit(solution)/shard_map/ppermute | solution.py:400
  25.9 37.0 %copy-start.2 = (bf16[128,1024]{1,0:T(8,128)(2,1)}, bf16[128,1024]{1,0:T(8,128)(2,1)S(1)}, u32[]{:S(2)}) copy-start(bf16[128,1024]{1,0:T(8,128)(2,1)S(1)} %collective-permute-done.1.refs_2_) | copy-start | bytes 786436
  33.4 29.5 %copy-start.4 = (bf16[128,1024]{1,0:T(8,128)(2,1)}, bf16[128,1024]{1,0:T(8,128)(2,1)S(1)}, u32[]{:S(2)}) copy-start(bf16[128,1024]{1,0:T(8,128)(2,1)S(1)} %collective-permute-done.2.refs_3_) | copy-start | bytes 786436
  33.4 26.8 %collective-permute-start.7 = (bf16[256,1024]{1,0:T(8,128)(2,1)}, bf16[256,1024]{1,0:T(8,128)(2,1)S(1)}, u32[]{:S(2)}, u32[]{:S(2)}) collective-permute-start(bf16[256,1024]{1,0:T(8,128)(2,1)} %x_near_ref.1), channel_id=1, source_target_pairs={{0,8},{2,10},{4,12},{6,14},{8,0},{10,2},{12,4},{14,6},{1,9},{3,11}... | collective-permute-start | bytes 1572872 | tf_op jit(solution)/shard_map/ppermute | solution.py:400
  35.3 29.4 %copy-start.6 = (bf16[128,1024]{1,0:T(8,128)(2,1)}, bf16[128,1024]{1,0:T(8,128)(2,1)S(1)}, u32[]{:S(2)}) copy-start(bf16[128,1024]{1,0:T(8,128)(2,1)S(1)} %get-tuple-element.73.refs_4_) | copy-start | bytes 786436
  35.3 6.7 %collective-permute-start.4 = (bf16[128,1024]{1,0:T(8,128)(2,1)S(1)}, bf16[128,1024]{1,0:T(8,128)(2,1)S(1)}, u32[]{:S(2)}, u32[]{:S(2)}) collective-permute-start(bf16[128,1024]{1,0:T(8,128)(2,1)S(1)} %get-tuple-element.65), channel_id=1, source_target_pairs={{0,2},{2,0},{4,6},{6,4},{8,10},{10,8},{12,14},{14,12},{1,3},{3,1},... | collective-permute-start | bytes 786440 | tf_op jit(solution)/shard_map/ppermute | solution.py:400
  36.2 16.0 %collective-permute-start.5 = (bf16[128,1024]{1,0:T(8,128)(2,1)S(1)}, bf16[128,1024]{1,0:T(8,128)(2,1)S(1)}, u32[]{:S(2)}, u32[]{:S(2)}) collective-permute-start(bf16[128,1024]{1,0:T(8,128)(2,1)S(1)} %get-tuple-element.66), channel_id=1, source_target_pairs={{0,4},{2,6},{4,0},{6,2},{8,12},{10,14},{12,8},{14,10},{1,5},{3,7},... | collective-permute-start | bytes 786440 | tf_op jit(solution)/shard_map/ppermute | solution.py:400
  39.2 20.3 %collective-permute-start.6 = (bf16[128,1024]{1,0:T(8,128)(2,1)S(1)}, bf16[128,1024]{1,0:T(8,128)(2,1)S(1)}, u32[]{:S(2)}, u32[]{:S(2)}) collective-permute-start(bf16[128,1024]{1,0:T(8,128)(2,1)S(1)} %get-tuple-element.67), channel_id=1, source_target_pairs={{0,6},{2,4},{4,2},{6,0},{8,14},{10,12},{12,10},{14,8},{1,7},{3,5},... | collective-permute-start | bytes 786440 | tf_op jit(solution)/shard_map/ppermute | solution.py:400
  41.9 24.5 %copy-start.8 = (bf16[128,1024]{1,0:T(8,128)(2,1)}, bf16[128,1024]{1,0:T(8,128)(2,1)S(1)}, u32[]{:S(2)}) copy-start(bf16[128,1024]{1,0:T(8,128)(2,1)S(1)} %collective-permute-done.4.refs_5_) | copy-start | bytes 786436
  52.2 0.7 copy-start.10
  59.5 0.7 copy-start.12
  60.2 1.0 copy-start
  62.9 17.5 %collective-permute-start.8 = (bf16[256,1024]{1,0:T(8,128)(2,1)}, bf16[256,1024]{1,0:T(8,128)(2,1)S(1)}, u32[]{:S(2)}, u32[]{:S(2)}) collective-permute-start(bf16[256,1024]{1,0:T(8,128)(2,1)} %get-tuple-element.78), channel_id=1, source_target_pairs={{0,2},{2,0},{4,6},{6,4},{8,10},{10,8},{12,14},{14,12},{1,3},{3,1},... | collective-permute-start | bytes 1572872 | tf_op jit(solution)/shard_map/ppermute | solution.py:400
  64.6 15.9 %collective-permute-start.9 = (bf16[256,1024]{1,0:T(8,128)(2,1)}, bf16[256,1024]{1,0:T(8,128)(2,1)S(1)}, u32[]{:S(2)}, u32[]{:S(2)}) collective-permute-start(bf16[256,1024]{1,0:T(8,128)(2,1)} %get-tuple-element.79), channel_id=1, source_target_pairs={{0,4},{2,6},{4,0},{6,2},{8,12},{10,14},{12,8},{14,10},{1,5},{3,7},... | collective-permute-start | bytes 1572872 | tf_op jit(solution)/shard_map/ppermute | solution.py:400
  64.6 23.6 %collective-permute-start.10 = (bf16[256,1024]{1,0:T(8,128)(2,1)}, bf16[256,1024]{1,0:T(8,128)(2,1)S(1)}, u32[]{:S(2)}, u32[]{:S(2)}) collective-permute-start(bf16[256,1024]{1,0:T(8,128)(2,1)} %get-tuple-element.80), channel_id=1, source_target_pairs={{0,6},{2,4},{4,2},{6,0},{8,14},{10,12},{12,10},{14,8},{1,7},{3,5},... | collective-permute-start | bytes 1572872 | tf_op jit(solution)/shard_map/ppermute | solution.py:400
  66.4 1.0 copy-start.3
  67.4 0.9 copy-start.5
  68.3 0.9 copy-start.7
  69.3 0.9 copy-start.9
  70.2 0.9 copy-start.11
  71.2 0.9 copy-start.13
  101.3 18.2 %collective-permute-start.14 = (bf16[8,128,2048]{2,1,0:T(8,128)(2,1)S(1)}, bf16[8,128,2048]{2,1,0:T(8,128)(2,1)S(1)}, u32[]{:S(2)}, u32[]{:S(2)}) collective-permute-start(bf16[8,128,2048]{2,1,0:T(8,128)(2,1)S(1)} %get-tuple-element.86.pack_ref), channel_id=1, source_target_pairs={{0,1},{1,0},{2,3},{3,2},{4,5},{5,4},{6,7},{7,6},{8,9},{9,8},{10,11... | collective-permute-start | bytes 12582920 | tf_op jit(solution)/shard_map/ppermute | solution.py:403
  101.4 12.8 %collective-permute-start.15 = (bf16[8,128,1024]{2,1,0:T(8,128)(2,1)S(1)}, bf16[8,128,1024]{2,1,0:T(8,128)(2,1)S(1)}, u32[]{:S(2)}, u32[]{:S(2)}) collective-permute-start(bf16[8,128,1024]{2,1,0:T(8,128)(2,1)S(1)} %get-tuple-element.92.d_ref), channel_id=1, source_target_pairs={{0,1},{1,0},{2,3},{3,2},{4,5},{5,4},{6,7},{7,6},{8,9},{9,8},{10,11... | collective-permute-start | bytes 6291464 | tf_op jit(solution)/shard_map/ppermute | solution.py:403
  101.9 5.8 %collective-permute-start.16 = (bf16[144,512]{1,0:T(8,128)(2,1)S(1)}, bf16[144,512]{1,0:T(8,128)(2,1)S(1)}, u32[]{:S(2)}, u32[]{:S(2)}) collective-permute-start(bf16[144,512]{1,0:T(8,128)(2,1)S(1)} %get-tuple-element.96), channel_id=1, source_target_pairs={{0,2},{2,0},{4,6},{6,4},{8,10},{10,8},{12,14},{14,12},{1,3},{3,1},... | collective-permute-start | bytes 442376 | tf_op jit(solution)/shard_map/ppermute | solution.py:400
  103.1 6.7 %collective-permute-start.17 = (bf16[144,512]{1,0:T(8,128)(2,1)S(1)}, bf16[144,512]{1,0:T(8,128)(2,1)S(1)}, u32[]{:S(2)}, u32[]{:S(2)}) collective-permute-start(bf16[144,512]{1,0:T(8,128)(2,1)S(1)} %get-tuple-element.97), channel_id=1, source_target_pairs={{0,4},{2,6},{4,0},{6,2},{8,12},{10,14},{12,8},{14,10},{1,5},{3,7},... | collective-permute-start | bytes 442376 | tf_op jit(solution)/shard_map/ppermute | solution.py:400
  103.4 9.9 %collective-permute-start.18 = (bf16[144,512]{1,0:T(8,128)(2,1)S(1)}, bf16[144,512]{1,0:T(8,128)(2,1)S(1)}, u32[]{:S(2)}, u32[]{:S(2)}) collective-permute-start(bf16[144,512]{1,0:T(8,128)(2,1)S(1)} %get-tuple-element.98), channel_id=1, source_target_pairs={{0,6},{2,4},{4,2},{6,0},{8,14},{10,12},{12,10},{14,8},{1,7},{3,5},... | collective-permute-start | bytes 442376 | tf_op jit(solution)/shard_map/ppermute | solution.py:400
  107.8 10.4 %collective-permute-start.11 = (bf16[128,512]{1,0:T(8,128)(2,1)S(1)}, bf16[128,512]{1,0:T(8,128)(2,1)S(1)}, u32[]{:S(2)}, u32[]{:S(2)}) collective-permute-start(bf16[128,512]{1,0:T(8,128)(2,1)S(1)} %get-tuple-element.83), channel_id=1, source_target_pairs={{0,2},{2,0},{4,6},{6,4},{8,10},{10,8},{12,14},{14,12},{1,3},{3,1},... | collective-permute-start | bytes 393224 | tf_op jit(solution)/shard_map/ppermute | solution.py:400
  109.9 8.3 %collective-permute-start.12 = (bf16[128,512]{1,0:T(8,128)(2,1)S(1)}, bf16[128,512]{1,0:T(8,128)(2,1)S(1)}, u32[]{:S(2)}, u32[]{:S(2)}) collective-permute-start(bf16[128,512]{1,0:T(8,128)(2,1)S(1)} %get-tuple-element.84), channel_id=1, source_target_pairs={{0,4},{2,6},{4,0},{6,2},{8,12},{10,14},{12,8},{14,10},{1,5},{3,7},... | collective-permute-start | bytes 393224 | tf_op jit(solution)/shard_map/ppermute | solution.py:400
  113.3 6.2 %collective-permute-start.13 = (bf16[128,512]{1,0:T(8,128)(2,1)S(1)}, bf16[128,512]{1,0:T(8,128)(2,1)S(1)}, u32[]{:S(2)}, u32[]{:S(2)}) collective-permute-start(bf16[128,512]{1,0:T(8,128)(2,1)S(1)} %get-tuple-element.85), channel_id=1, source_target_pairs={{0,6},{2,4},{4,2},{6,0},{8,14},{10,12},{12,10},{14,8},{1,7},{3,5},... | collective-permute-start | bytes 393224 | tf_op jit(solution)/shard_map/ppermute | solution.py:400
  114.7 19.3 %collective-permute-start.19 = (bf16[320,512]{1,0:T(8,128)(2,1)S(1)}, bf16[320,512]{1,0:T(8,128)(2,1)S(1)}, u32[]{:S(2)}, u32[]{:S(2)}) collective-permute-start(bf16[320,512]{1,0:T(8,128)(2,1)S(1)} %relay_sum.3), channel_id=1, source_target_pairs={{0,8},{2,10},{4,12},{6,14},{8,0},{10,2},{12,4},{14,6},{1,9},{3,11}... | collective-permute-start | bytes 983048 | tf_op jit(solution)/shard_map/ppermute | solution.py:400
  120.0 22.0 %collective-permute-start.21 = (bf16[144,1024]{1,0:T(8,128)(2,1)S(1)}, bf16[144,1024]{1,0:T(8,128)(2,1)S(1)}, u32[]{:S(2)}, u32[]{:S(2)}) collective-permute-start(bf16[144,1024]{1,0:T(8,128)(2,1)S(1)} %get-tuple-element.108), channel_id=1, source_target_pairs={{0,2},{2,0},{4,6},{6,4},{8,10},{10,8},{12,14},{14,12},{1,3},{3,1},... | collective-permute-start | bytes 884744 | tf_op jit(solution)/shard_map/ppermute | solution.py:400
  121.2 20.8 %collective-permute-start.22 = (bf16[144,1024]{1,0:T(8,128)(2,1)S(1)}, bf16[144,1024]{1,0:T(8,128)(2,1)S(1)}, u32[]{:S(2)}, u32[]{:S(2)}) collective-permute-start(bf16[144,1024]{1,0:T(8,128)(2,1)S(1)} %get-tuple-element.109), channel_id=1, source_target_pairs={{0,4},{2,6},{4,0},{6,2},{8,12},{10,14},{12,8},{14,10},{1,5},{3,7},... | collective-permute-start | bytes 884744 | tf_op jit(solution)/shard_map/ppermute | solution.py:400
  122.3 22.2 %collective-permute-start.23 = (bf16[144,1024]{1,0:T(8,128)(2,1)S(1)}, bf16[144,1024]{1,0:T(8,128)(2,1)S(1)}, u32[]{:S(2)}, u32[]{:S(2)}) collective-permute-start(bf16[144,1024]{1,0:T(8,128)(2,1)S(1)} %get-tuple-element.110), channel_id=1, source_target_pairs={{0,6},{2,4},{4,2},{6,0},{8,14},{10,12},{12,10},{14,8},{1,7},{3,5},... | collective-permute-start | bytes 884744 | tf_op jit(solution)/shard_map/ppermute | solution.py:400
  123.5 18.5 %collective-permute-start.20 = (bf16[256,512]{1,0:T(8,128)(2,1)S(1)}, bf16[256,512]{1,0:T(8,128)(2,1)S(1)}, u32[]{:S(2)}, u32[]{:S(2)}) collective-permute-start(bf16[256,512]{1,0:T(8,128)(2,1)S(1)} %relay_sum.2), channel_id=1, source_target_pairs={{0,8},{2,10},{4,12},{6,14},{8,0},{10,2},{12,4},{14,6},{1,9},{3,11}... | collective-permute-start | bytes 786440 | tf_op jit(solution)/shard_map/ppermute | solution.py:400
where the time goes:
time: 147 us; the launch traced here: 146 us
  waiting for transfers between devices  67.6 us (46%)
  Pallas kernels  35.7 us (24%)
  starting transfers between devices  31.6 us (21%)
  local copies, waits for them, and re-layouts  10.6 us (7%)
    ppermute x22, waiting for transfers between devices, swap(): return lax.ppermute(value, 'expert', [(i, i ^ m) for i in range(chips)])  67.5 us
    ppermute x22, starting transfers between devices, swap(): return lax.ppermute(value, 'expert', [(i, i ^ m) for i in range(chips)])  31.1 us
    pallas_call x1, Pallas kernels, up_pass(): pl.pallas_call(functools.partial(up_kernel, peers), out_shape=[jax.ShapeD...  13.2 us
    unnamed x32, local copies, waits for them, and re-layouts  10.6 us
    pallas_call x1, Pallas kernels, down_pass(): pl.pallas_call(functools.partial(down_kernel, peers), out_shape=[jax.Shap...  8.33 us
    pallas_call x1, Pallas kernels, weight_pass(): pl.pallas_call(weight_kernel, grid=(experts,), out_shape=[jax.ShapeDtypeS...  7.91 us
  transfers between devices with their start and end apart: 24, of which 13 were waited for; matrix products, arithmetic and copies ran while one was open for 0% of the time, Pallas kernels for 13%

commit v1 on v0

v1 whole, which is shorter than its diff:
```python
import functools

import jax
import jax.numpy as jnp
from jax import lax
from jax.experimental import pallas as pl
from jax.experimental.pallas import tpu as pltpu
from jax.sharding import PartitionSpec as P

EXPERTS = 64
CAP = 16
BF = jnp.bfloat16
F32 = jnp.float32
NT = (((1,), (1,)), ((), ()))
NN = (((1,), (0,)), ((), ()))
TN = (((0,), (0,)), ((), ()))


def dot(a, b, dims, precision=None):
    return lax.dot_general(a, b, dims, preferred_element_type=F32, precision=precision)


COST = pl.CostEstimate(flops=1 << 20, bytes_accessed=1 << 20, transcendentals=0)


def params(mebibytes=14):
    return pltpu.CompilerParams(vmem_limit_bytes=mebibytes * 1024 * 1024)


def targets(routes):
    tokens = routes.shape[1]
    first, second = routes[0:1, :], routes[1:2, :]
    experts = lax.broadcasted_iota(jnp.int32, (EXPERTS, tokens), 0)
    one = (experts == first).astype(F32)
    two = (experts == second).astype(F32)
    earlier = lax.broadcasted_iota(jnp.int32, (tokens, tokens), 0) < lax.broadcasted_iota(
        jnp.int32, (tokens, tokens), 1
    )
    before = dot((one + two).astype(BF), earlier.astype(F32).astype(BF), NN)
    rank_one = jnp.sum(one * before, axis=0, keepdims=True).astype(jnp.int32)
    rank_two = jnp.sum(two * (before + one), axis=0, keepdims=True).astype(jnp.int32)
    return first * CAP + rank_one, second * CAP + rank_two


def thirds(value):
    high = value.astype(BF)
    rest = value - high.astype(F32)
    mid = rest.astype(BF)
    return [high, mid, (rest - mid.astype(F32)).astype(BF)]


def added(rows):
    rows = rows.astype(F32)
    return rows[0:1, :] + rows[1:2, :] + rows[2:3, :]


IN_HBM = pl.BlockSpec(memory_space=pltpu.HBM)


def in_hbm(value):
    return pltpu.with_memory_space_constraint(value, pltpu.HBM)


def prepare_kernel(routes_hbm, gates_hbm, g_hbm, x_hbm, out_ref, x_ref, routes_ref, gates_ref, sem):
    tokens, width = g_hbm.shape
    copies = [
        pltpu.make_async_copy(routes_hbm, routes_ref, sem.at[0]),
        pltpu.make_async_copy(gates_hbm, gates_ref, sem.at[1]),
        pltpu.make_async_copy(g_hbm, out_ref.at[0:tokens], sem.at[2]),
        pltpu.make_async_copy(x_hbm, x_ref, sem.at[3]),
    ]
    for copy in copies:
        copy.start()
    out_ref[tokens:, tokens:] = jnp.zeros((CAP, width - tokens), BF)
    copies[0].wait()
    copies[1].wait()
    routes = routes_ref[...].astype(F32).astype(BF)
    gates = gates_ref[...]
    rows = [routes, *thirds(gates[0:1, :]), *thirds(gates[1:2, :]), jnp.zeros((CAP - 8, tokens), BF)]
    out_ref[tokens:, 0:tokens] = jnp.concatenate(rows, axis=0)
    copies[2].wait()
    copies[3].wait()


def prepare(routes, gates, g, x):
    tokens, width = g.shape
    return pl.pallas_call(
        prepare_kernel,
        out_shape=[jax.ShapeDtypeStruct((tokens + CAP, width), BF), jax.ShapeDtypeStruct(x.shape, BF)],
        in_specs=[IN_HBM] * 4,
        out_specs=[pl.BlockSpec(memory_space=pltpu.VMEM)] * 2,
        scratch_shapes=[
            pltpu.VMEM(routes.shape, jnp.int32),
            pltpu.VMEM(gates.shape, F32),
            pltpu.SemaphoreType.DMA((4,)),
        ],
        compiler_params=params(),
        cost_estimate=COST,
        name="prepare",
    )(in_hbm(routes), in_hbm(gates), in_hbm(g), in_hbm(x))


def facts_of(g_ref, tokens):
    facts = g_ref[tokens : tokens + 8, 0:tokens]
    return targets(facts[0:2, :].astype(F32).astype(jnp.int32)), (added(facts[2:5, :]), added(facts[5:8, :]))


def select_slots(targets_of, gates, base, slots):
    rows = lax.broadcasted_iota(jnp.int32, (slots, targets_of[0].shape[1]), 0) + base
    is_one, is_two = rows == targets_of[0], rows == targets_of[1]
    gate = jnp.where(is_one, gates[0], 0.0) + jnp.where(is_two, gates[1], 0.0)
    return jnp.where(is_one | is_two, 1.0, 0.0).astype(BF), jnp.sum(gate, axis=1, keepdims=True)


def whole(*shape):
    return pl.BlockSpec(shape, lambda j: (0,) * len(shape), pipeline_mode=pl.Buffered(1))


def by_expert(*shape):
    return pl.BlockSpec(shape, lambda j: (j,) + (0,) * (len(shape) - 1))


def rows_kernel(peers, parts, me_ref, g_ref, x_ref, select_ref, facts_ref, *rows_refs):
    slots, tokens = select_ref.shape[1:]
    size = slots // parts
    tgt, gates = facts_of(g_ref, tokens)
    for m in range(peers):
        select, gate = select_slots(tgt, gates, (me_ref[0] ^ m) * slots, slots)
        select_ref[m] = select
        x = dot(select, x_ref[...], NN).astype(BF)
        d = (gate * dot(select, g_ref[0:tokens], NN)).astype(BF)
        for i in range(parts):
            rows_refs[i * peers + m][0:size] = x[i * size : (i + 1) * size]
            rows_refs[i * peers + m][size:] = d[i * size : (i + 1) * size]
    facts_ref[0:2] = jnp.concatenate(tgt, axis=0).astype(F32)
    facts_ref[2:4] = jnp.concatenate(gates, axis=0)
    facts_ref[4:8] = jnp.zeros((4, tokens), F32)


SCALARS = pl.BlockSpec(memory_space=pltpu.SMEM)
VECTORS = pl.BlockSpec(memory_space=pltpu.VMEM)


def rows_pass(name, parts, me, g, x, peers, slots):
    tokens, width = x.shape
    out = pl.pallas_call(
        functools.partial(rows_kernel, peers, parts),
        out_shape=[jax.ShapeDtypeStruct((peers, slots, tokens), BF), jax.ShapeDtypeStruct((8, tokens), F32)]
        + [jax.ShapeDtypeStruct((2 * slots // parts, width), BF)] * (parts * peers),
        in_specs=[SCALARS] + [VECTORS] * 2,
        out_specs=[VECTORS] * (2 + parts * peers),
        compiler_params=params(),
        cost_estimate=COST,
        name=name,
    )(me, g, x)
    return out[0], out[1], *(list(out[2 + i * peers : 2 + (i + 1) * peers]) for i in range(parts))


def fetch(weight_hbm, weight_ref, sem, first=0):
    copies = [
        pltpu.make_async_copy(weight_hbm.at[first + j], weight_ref.at[j], sem.at[j])
        for j in range(weight_ref.shape[0])
    ]
    for copy in copies:
        copy.start()
    return copies


def turn_kernel(weight_ref, out_ref):
    out_ref[0] = weight_ref[0].T


def turned(weight):
    experts, hidden, width = weight.shape
    return pl.pallas_call(
        turn_kernel,
        grid=(experts,),
        out_shape=pltpu.HBM((experts, width, hidden), weight.dtype),
        in_specs=[by_expert(1, hidden, width)],
        out_specs=by_expert(1, width, hidden),
        compiler_params=params(),
        cost_estimate=COST,
        name="turned",
    )(in_hbm(weight))


def joined(parts):
    return jnp.concatenate(parts, axis=0)


def of_expert(j, first=0):
    return slice(first + j * CAP, first + (j + 1) * CAP)


def block_kernel(peers, which, core_ref, up_hbm, down_hbm, *refs):
    def take(n):
        nonlocal refs
        taken, refs = refs[:n], refs[n:]
        return taken

    near_refs, far_refs = take(peers), take(peers)
    early_part, _ = (take(1), take(2)) if which else ((), ())
    gx_refs, part_out = take((1 + which) * peers), take(1 - which)
    pack_hbm, mine_hbm, up_ref, down_ref = take(4)
    part_ref = take(1)[0] if which else part_out[0]
    pack_ref, mine_ref, in_sem, out_sem = refs
    experts = up_ref.shape[0]
    width = far_refs[0].shape[1]
    slots, half, count = experts * CAP, mine_ref.shape[2] // 2, 2 * peers * CAP
    core = core_ref[0]

    def store(j):
        return (
            pltpu.make_async_copy(pack_ref.at[j], pack_hbm.at[which * experts + j], out_sem.at[j, 0]),
            pltpu.make_async_copy(mine_ref.at[j], mine_hbm.at[which * experts + j], out_sem.at[j, 1]),
        )

    def rows_of(j, kind):
        near, far = (2 * kind + which) * slots + j * CAP, kind * slots + j * CAP
        return joined([ref[near : near + CAP] for ref in near_refs] + [ref[far : far + CAP] for ref in far_refs])

    weights = ((up_hbm, up_ref), (down_hbm, down_ref))
    copies = [
        [
            pltpu.make_async_copy(hbm.at[which * experts + j], ref.at[j], in_sem.at[j, i])
            for i, (hbm, ref) in enumerate(weights)
        ]
        for j in range(experts)
    ]
    for group in copies:
        for copy in group:
            copy.start()

    def before(j):
        copies[j][0].wait()
        copies[j][1].wait()
        x, d = rows_of(j, 0), rows_of(j, 1)
        pack_ref[j, :, 0:width] = x
        pack_ref[j, :, width : 2 * width] = d
        return dot(x, up_ref[j], NN), dot(d, down_ref[j], NN)

    following = before(0)
    for j in range(experts):
        pre, h = following
        following = before(j + 1) if j + 1 < experts else None
        sig = 1.0 / (1.0 + jnp.exp(-pre))
        active = (pre * sig).astype(BF)
        grad_pre = (h * sig * (1.0 + pre * (1.0 - sig))).astype(BF)
        gx = dot(grad_pre, up_ref[j], NT).astype(BF)
        prod = active.astype(F32) * h
        part = prod[:, 0:128]
        for i in range(1, prod.shape[1] // 128):
            part = part + prod[:, i * 128 : (i + 1) * 128]
        for m in range(2 * peers):
            mine, to = slice(m * CAP, (m + 1) * CAP), j * CAP
            part_ref[m, to : to + CAP] = part[mine]
            if which:
                gx_refs[m][to : to + CAP] = gx[mine]
            else:
                to = to + m // peers * slots
                gx_refs[m % peers][to : to + CAP] = gx[mine]
        for i, value in enumerate((active, grad_pre)):
            low, high = value[:, 0:half], value[:, half:]
            to = i * half
            mine_ref[j, :, to : to + half] = jnp.where(core == 0, low, high)
            pack_ref[j, :, 2 * width + to : 2 * width + to + half] = jnp.where(core == 0, high, low)
        for out in store(j):
            out.start()
    if which:
        for m in range(2 * peers):
            total = jnp.sum(joined([early_part[0][m], part_ref[m]]).T, axis=0, keepdims=True)
            gx_refs[m][slots:, 0 : 2 * slots] = joined([*thirds(total), jnp.zeros((CAP - 3, 2 * slots), BF)])
            gx_refs[m][slots:, 2 * slots :] = jnp.zeros((CAP, width - 2 * slots), BF)
    for j in range(experts):
        for out in store(j):
            out.wait()


def block_pass(which, core, up, down, near, far, early=()):
    experts, width, hidden = up.shape[0] // 2, *up.shape[1:]
    peers = len(near)
    count, slots = 2 * peers * CAP, experts * CAP
    pack, mine, part = (experts, count, 2 * width + hidden), (experts, count, hidden), (2 * peers, slots, 128)
    gx = [(slots + CAP, width)] * (2 * peers) if which else [(2 * slots, width)] * peers
    anywhere = pl.BlockSpec(memory_space=pl.ANY)
    out = pl.pallas_call(
        functools.partial(block_kernel, peers, which),
        out_shape=[jax.ShapeDtypeStruct(shape, BF) for shape in gx]
        + ([] if which else [jax.ShapeDtypeStruct(part, F32)])
        + [jax.ShapeDtypeStruct((2 * experts, *shape[1:]), BF) for shape in (pack, mine)],
        in_specs=[SCALARS] + [IN_HBM] * 2 + [VECTORS] * (2 * peers + which) + [anywhere] * (2 * which),
        out_specs=[VECTORS] * (len(gx) + 1 - which) + [anywhere] * 2,
        scratch_shapes=[pltpu.VMEM((experts, width, hidden), BF)] * 2
        + [pltpu.VMEM(part, F32)] * which
        + [
            pltpu.VMEM(pack, BF),
            pltpu.VMEM(mine, BF),
            pltpu.SemaphoreType.DMA((experts, 2)),
            pltpu.SemaphoreType.DMA((experts, 2)),
        ],
        input_output_aliases={4 + 2 * peers + i: len(gx) + i for i in range(2 * which)},
        compiler_params=params(26),
        cost_estimate=COST,
        name=("first_experts", "last_experts")[which],
    )(core, in_hbm(up), in_hbm(down), *near, *far, *early)
    return list(out[: len(gx)]), *out[len(gx) :]


def weight_kernel(mine_ref, pack_ref, other_ref, up_ref, down_ref):
    half, width = up_ref.shape[1:]
    active = joined([mine_ref[0, :, 0:half], other_ref[0, :, 2 * width : 2 * width + half]])
    grad_pre = joined([mine_ref[0, :, half:], other_ref[0, :, 2 * width + half :]])
    x, d = (joined([ref[0, :, i * width : (i + 1) * width] for ref in (pack_ref, other_ref)]) for i in range(2))
    up_ref[0] = dot(grad_pre, x, TN).astype(BF)
    down_ref[0] = dot(active, d, TN).astype(BF)


def weight_pass(mine, pack, other):
    experts, rows, hidden = mine.shape
    width = (pack.shape[2] - hidden) // 2
    return pl.pallas_call(
        weight_kernel,
        grid=(experts,),
        out_shape=[jax.ShapeDtypeStruct((experts, hidden // 2, width), BF)] * 2,
        in_specs=[by_expert(1, rows, n) for n in (hidden, 2 * width, 2 * width + hidden)],
        out_specs=[by_expert(1, hidden // 2, width)] * 2,
        compiler_params=params(),
        cost_estimate=COST,
        name="weight_pass",
    )(mine, pack, other)


def tail_rows(peers):
    return -(-3 * peers // CAP) * CAP


def relay_kernel(peers, select_ref, *refs):
    early_refs, late_refs, out_ref = refs[:peers], refs[peers : 2 * peers], refs[2 * peers]
    slots, tokens = select_ref.shape[1:]
    half, width = slots // 2, out_ref.shape[1]
    total = None
    for m in range(peers):
        term = dot(select_ref[m, 0:half], early_refs[m][half:], TN) + dot(
            select_ref[m, half:], late_refs[m][0:half], TN
        )
        total = term if total is None else total + term
    out_ref[0:tokens] = total.astype(BF)
    tails = [ref[half : half + 3] for ref in late_refs]
    out_ref[tokens:] = joined([*tails, jnp.zeros((tail_rows(peers) - 3 * peers, width), BF)])


def relay_pass(select, early, late):
    peers, slots, tokens = select.shape
    return pl.pallas_call(
        functools.partial(relay_kernel, peers),
        out_shape=jax.ShapeDtypeStruct((tokens + tail_rows(peers), early[0].shape[1]), BF),
        in_specs=[VECTORS] * (1 + 2 * peers),
        out_specs=VECTORS,
        compiler_params=params(),
        cost_estimate=COST,
        name="relay_sum",
    )(select, *early, *late)


def slot_values(tgt, chip, tail, slots):
    at = lax.broadcasted_iota(jnp.int32, (slots, tgt[0].shape[1]), 0) + chip * slots
    column = added(tail).T
    return [jnp.sum(jnp.where(at == t, column, 0.0), axis=0, keepdims=True) for t in tgt]


def targets_in(facts_ref):
    return facts_ref[0:1, :].astype(jnp.int32), facts_ref[1:2, :].astype(jnp.int32)


def near_sum_kernel(me_ref, facts_ref, select_ref, *refs):
    peers, slots, tokens = select_ref.shape
    early_refs, late_refs, (out_ref, gates_ref) = refs[:peers], refs[peers : 2 * peers], refs[2 * peers :]
    half = slots // 2
    tgt = targets_in(facts_ref)
    total, values = None, [jnp.zeros((1, tokens), F32)] * 2
    for m in range(peers):
        term = dot(select_ref[m, 0:half], early_refs[m][0:half], TN) + dot(
            select_ref[m, half:], late_refs[m][0:half], TN
        )
        total = term if total is None else total + term
        more = slot_values(tgt, me_ref[0] ^ m, late_refs[m][half : half + CAP, 0:slots], slots)
        values = [value + new for value, new in zip(values, more)]
    out_ref[...] = total.astype(BF)
    gates_ref[...] = joined(values)


def near_sum(me, facts, select, early, late):
    tokens, width = select.shape[2], early[0].shape[1]
    return pl.pallas_call(
        near_sum_kernel,
        out_shape=[jax.ShapeDtypeStruct((tokens, width), BF), jax.ShapeDtypeStruct((2, tokens), F32)],
        in_specs=[SCALARS] + [VECTORS] * (2 + 2 * len(early)),
        out_specs=[VECTORS] * 2,
        compiler_params=params(),
        cost_estimate=COST,
        name="near_sum",
    )(me, facts, select, *early, *late)


def last_kernel(peers, me_ref, facts_ref, near_ref, values_ref, back_ref, out_ref, gates_ref):
    tokens = near_ref.shape[0]
    slots = EXPERTS // (2 * peers) * CAP
    tgt = targets_in(facts_ref)
    values = [values_ref[k : k + 1, :] for k in range(2)]
    for m in range(peers):
        tail = back_ref[tokens:, 0:slots].astype(F32)[3 * m : 3 * m + 3]
        more = slot_values(tgt, me_ref[0] ^ (peers + m), tail, slots)
        values = [value + new for value, new in zip(values, more)]
    gates_ref[...] = joined(values) / facts_ref[2:4, :]
    out_ref[...] = (near_ref[...].astype(F32) + back_ref[0:tokens].astype(F32)).astype(BF)


def last_pass(peers, me, facts, near, values, back):
    return pl.pallas_call(
        functools.partial(last_kernel, peers),
        out_shape=[jax.ShapeDtypeStruct(near.shape, BF), jax.ShapeDtypeStruct(values.shape, F32)],
        in_specs=[SCALARS] + [VECTORS] * 4,
        out_specs=[VECTORS] * 2,
        compiler_params=params(),
        cost_estimate=COST,
        name="last_sum",
    )(me, facts, near, values, back)


def after(value, *others):
    return lax.optimization_barrier((value, *others))[0]


def per_device(tokens, routes, gate_values, up_weight, down_weight, grad_out):
    chips = lax.axis_size("expert")
    half = chips // 2
    slots = up_weight.shape[0] * CAP
    me = lax.axis_index("expert").astype(jnp.int32).reshape(1)
    core = lax.axis_index("dp").astype(jnp.int32).reshape(1)

    def swap(value, m):
        return lax.ppermute(value, "expert", [(i, i ^ m) for i in range(chips)])

    def swap_core(value):
        return lax.ppermute(value, "dp", [(0, 1), (1, 0)])

    def deal(rows):
        return [rows[0]] + [swap(rows[m], m) for m in range(1, half)]

    g_near, x_near = prepare(routes.T, gate_values.T, grad_out, tokens)
    g_far = swap(g_near, half)
    x_far = swap(tokens, half)
    select, facts, near = rows_pass("near_rows", 1, me, g_near, x_near, half, slots)
    near = deal(near)
    weights = turned(up_weight), turned(down_weight)
    select_far, _, far_first, far_last = rows_pass(
        "far_rows", 2, me, after(g_far, near, weights), x_far, half, slots
    )
    far_first = deal(far_first)
    far_last = deal(after(far_last, far_first[1]))

    gx_first, part, pack, mine = block_pass(0, core, *weights, near, far_first)
    gx_first = deal(gx_first)
    gx_last, pack, mine = block_pass(1, core, *weights, near, far_last, (part, pack, mine))
    relay = relay_pass(select_far, gx_first, deal(gx_last[half:]))
    back = swap(relay, half)
    other = swap_core(after(pack, relay))
    near_last = deal(after(gx_last[:half], relay))

    grad_up, grad_down = weight_pass(mine, pack, other)
    near_tokens, near_gates = near_sum(me, after(facts, grad_up), select, gx_first, near_last)
    grad_tokens, grad_gates = last_pass(half, me, facts, near_tokens, near_gates, after(back, near_tokens))
    return grad_tokens, grad_gates.T, grad_up, grad_down


def solution(mesh):
    placed = (
        P(("group", "expert", "dp"), None),
        P(("group", "expert", "dp"), None),
        P(("group", "expert", "dp"), None),
        P("expert", None, None),
        P("expert", None, None),
        P(("group", "expert", "dp"), None),
    )
    return jax.shard_map(
        per_device,
        mesh=mesh,
        in_specs=placed,
        out_specs=(
            P(("group", "expert", "dp"), None),
            P(("group", "expert", "dp"), None),
            P(("group", "expert"), "dp", None),
            P(("group", "expert"), "dp", None),
        ),
        check_vma=False,
    )
```

time: 147 us -> 138 us (0.939)
  Pallas kernels: 35.7 us -> 66.4 us
  waiting for transfers between devices: 67.6 us -> 40.3 us
  local copies, waits for them, and re-layouts: 10.6 us -> 2.36 us
  starting transfers between devices: 31.6 us -> 27.5 us
    ppermute x22 -> x21, waiting for transfers between devices: 67.5 us -> 35.8 us  [swap(): return lax.ppermute(value, 'expert', [(i, i ^ m) for i in range(chips)])]
    pallas_call x7 -> x9, Pallas kernels: 26.9 us -> 57.1 us  [the longest x2 30.9 us: turned(): pl.pallas_call(turn_kernel, grid=(experts,), out_shape=pltpu.HBM((experts...]
    unnamed x32 -> x12, local copies, waits for them, and re-layouts: 10.6 us -> 2.36 us
    ppermute x2 -> x1, waiting for transfers between devices: 0.01 us -> 4.45 us  [swap_core(): return lax.ppermute(value, 'dp', [(0, 1), (1, 0)])]
    ppermute x22 -> x21, starting transfers between devices: 31.1 us -> 27.4 us  [swap(): return lax.ppermute(value, 'expert', [(i, i ^ m) for i in range(chips)])]
  transfers between devices with their start and end apart: 24 -> 22, of which waited for: 13 -> 11; matrix products, arithmetic and copies ran while one was open for 0% -> 0% of each run, Pallas kernels for 13% -> 44%
where the time goes in v1:
time: 138 us; the launch traced here: 137 us
  Pallas kernels  66.4 us (48%)
  waiting for transfers between devices  40.3 us (29%)
  starting transfers between devices  27.5 us (20%)
  local copies, waits for them, and re-layouts  2.36 us (2%)
    ppermute x21, waiting for transfers between devices, swap(): return lax.ppermute(value, 'expert', [(i, i ^ m) for i in range(chips)])  35.8 us
    pallas_call x2, Pallas kernels, turned(): pl.pallas_call(turn_kernel, grid=(experts,), out_shape=pltpu.HBM((experts...  30.9 us
    ppermute x21, starting transfers between devices, swap(): return lax.ppermute(value, 'expert', [(i, i ^ m) for i in range(chips)])  27.4 us
    pallas_call x2, Pallas kernels, block_pass(): pl.pallas_call(functools.partial(block_kernel, peers, which), out_shape=[...  19.4 us
    pallas_call x1, Pallas kernels, weight_pass(): pl.pallas_call(weight_kernel, grid=(experts,), out_shape=[jax.ShapeDtypeS...  8.05 us
    ppermute x1, waiting for transfers between devices, swap_core(): return lax.ppermute(value, 'dp', [(0, 1), (1, 0)])  4.45 us
    pallas_call x2, Pallas kernels, rows_pass(): pl.pallas_call(functools.partial(rows_kernel, peers, parts), out_shape=[j...  2.8 us
  transfers between devices with their start and end apart: 22, of which 11 were waited for; matrix products, arithmetic and copies ran while one was open for 0% of the time, Pallas kernels for 44%

profile of v1, /device:TPU:0, one launch (start us, length us, event | category | flops | bytes accessed | tf_op | source)
XLA Modules:
  0.0 137.2 jit_solution(10297916214645874346)
XLA Ops:
  0.6 1.3 prepare.1
  1.9 4.1 %collective-permute-start.3 = (bf16[272,1024]{1,0:T(8,128)(2,1)S(1)}, bf16[272,1024]{1,0:T(8,128)(2,1)S(1)}, u32[]{:S(2)}, u32[]{:S(2)}) collective-permute-start(bf16[272,1024]{1,0:T(8,128)(2,1)S(1)} %get-tuple-element.56.g_ref), channel_id=1, source_target_pairs={{0,8},{2,10},{4,12},{6,14},{8,0},{10,2},{12,4},{14,6},{1,9},{3,11}... | collective-permute-start | bytes 1671176 | tf_op jit(solution)/shard_map/ppermute | solution.py:442
  6.0 1.0 near_rows.1
  7.0 0.0 copy-start.2
  7.0 1.6 %collective-permute-start = (bf16[256,1024]{1,0:T(8,128)(2,1)S(1)}, bf16[256,1024]{1,0:T(8,128)(2,1)S(1)}, u32[]{:S(2)}, u32[]{:S(2)}) collective-permute-start(bf16[256,1024]{1,0:T(8,128)(2,1)S(1)} %get-tuple-element.60), channel_id=1, source_target_pairs={{0,2},{2,0},{4,6},{6,4},{8,10},{10,8},{12,14},{14,12},{1,3},{3,1},... | collective-permute-start | bytes 1572872 | tf_op jit(solution)/shard_map/ppermute | solution.py:442
  8.6 1.6 %collective-permute-start.1 = (bf16[256,1024]{1,0:T(8,128)(2,1)S(1)}, bf16[256,1024]{1,0:T(8,128)(2,1)S(1)}, u32[]{:S(2)}, u32[]{:S(2)}) collective-permute-start(bf16[256,1024]{1,0:T(8,128)(2,1)S(1)} %get-tuple-element.61), channel_id=1, source_target_pairs={{0,4},{2,6},{4,0},{6,2},{8,12},{10,14},{12,8},{14,10},{1,5},{3,7},... | collective-permute-start | bytes 1572872 | tf_op jit(solution)/shard_map/ppermute | solution.py:442
  10.2 0.4 collective-permute-start.2
  10.6 0.0 collective-permute-start.4
  10.6 15.5 %turned.2.up_hbm = bf16[8,1024,1024]{2,1,0:T(8,128)(2,1)} custom-call(bf16[8,1024,1024]{2,1,0:T(8,128)(2,1)} %weight_ref.2), custom_call_target="tpu_custom_call" | custom-call | flops 1048576 | bytes 1048576 | tf_op jit(solution)/shard_map/turned/pallas_call | solution.py:175
  26.1 15.5 %turned.3.down_hbm = bf16[8,1024,1024]{2,1,0:T(8,128)(2,1)} custom-call(bf16[8,1024,1024]{2,1,0:T(8,128)(2,1)} %weight_ref.3), custom_call_target="tpu_custom_call" | custom-call | flops 1048576 | bytes 1048576 | tf_op jit(solution)/shard_map/turned/pallas_call | solution.py:175
  41.5 4.0 %collective-permute-done.1.refs_2_ = bf16[256,1024]{1,0:T(8,128)(2,1)S(1)} collective-permute-done((bf16[256,1024]{1,0:T(8,128)(2,1)S(1)}, bf16[256,1024]{1,0:T(8,128)(2,1)S(1)}, u32[]{:S(2)}, u32[]{:S(2)}) %collective-permute-start.1) | collective-permute-done | bytes 524320 | tf_op jit(solution)/shard_map/ppermute | solution.py:442
  45.5 9.5 %collective-permute-done.2.refs_3_ = bf16[256,1024]{1,0:T(8,128)(2,1)S(1)} collective-permute-done((bf16[256,1024]{1,0:T(8,128)(2,1)S(1)}, bf16[256,1024]{1,0:T(8,128)(2,1)S(1)}, u32[]{:S(2)}, u32[]{:S(2)}) %collective-permute-start.2) | collective-permute-done | bytes 524320 | tf_op jit(solution)/shard_map/ppermute | solution.py:442
  55.0 0.0 collective-permute-done.3.g_ref
  55.0 0.0 collective-permute-done.4.x_ref
  55.0 1.8 %far_rows.1 = (bf16[4,128,256]{2,1,0:T(8,128)(2,1)S(1)}, f32[8,256]{1,0:T(8,128)}, bf16[128,1024]{1,0:T(8,128)(2,1)S(1)}, bf16[128,1024]{1,0:T(8,128)(2,1)S(1)},...) custom-call(s32[1]{0:T(128)} %bitcast.me_ref, ...), custom_call_target="tpu_custom_call" | custom-call | flops 1048576 | bytes 1048576 | tf_op jit(solution)/shard_map/far_rows/pallas_call | solution.py:146
  56.8 0.7 copy-done.4
  57.4 1.5 %collective-permute-start.5 = (bf16[128,1024]{1,0:T(8,128)(2,1)S(1)}, bf16[128,1024]{1,0:T(8,128)(2,1)S(1)}, u32[]{:S(2)}, u32[]{:S(2)}) collective-permute-start(bf16[128,1024]{1,0:T(8,128)(2,1)S(1)} %get-tuple-element.68), channel_id=1, source_target_pairs={{0,2},{2,0},{4,6},{6,4},{8,10},{10,8},{12,14},{14,12},{1,3},{3,1},... | collective-permute-start | bytes 786440 | tf_op jit(solution)/shard_map/ppermute | solution.py:442
  58.9 0.0 collective-permute-start.9
  58.9 2.0 %collective-permute-start.10 = (bf16[128,1024]{1,0:T(8,128)(2,1)}, bf16[128,1024]{1,0:T(8,128)(2,1)}, u32[]{:S(2)}, u32[]{:S(2)}) collective-permute-start(bf16[128,1024]{1,0:T(8,128)(2,1)} %get-tuple-element.75), channel_id=1, source_target_pairs={{0,6},{2,4},{4,2},{6,0},{8,14},{10,12},{12,10},{14,8},{1,7},{3,5},... | collective-permute-start | bytes 786440 | tf_op jit(solution)/shard_map/ppermute | solution.py:442
  60.9 5.1 %collective-permute-done.5.refs_5_ = bf16[128,1024]{1,0:T(8,128)(2,1)S(1)} collective-permute-done((bf16[128,1024]{1,0:T(8,128)(2,1)S(1)}, bf16[128,1024]{1,0:T(8,128)(2,1)S(1)}, u32[]{:S(2)}, u32[]{:S(2)}) %collective-permute-start.5) | collective-permute-done | bytes 262176 | tf_op jit(solution)/shard_map/ppermute | solution.py:442
  66.1 0.7 copy-done
  66.8 1.5 %collective-permute-start.6 = (bf16[128,1024]{1,0:T(8,128)(2,1)}, bf16[128,1024]{1,0:T(8,128)(2,1)S(1)}, u32[]{:S(2)}, u32[]{:S(2)}) collective-permute-start(bf16[128,1024]{1,0:T(8,128)(2,1)} %get-tuple-element.70), channel_id=1, source_target_pairs={{0,2},{2,0},{4,6},{6,4},{8,10},{10,8},{12,14},{14,12},{1,3},{3,1},... | collective-permute-start | bytes 786440 | tf_op jit(solution)/shard_map/ppermute | solution.py:442
  68.2 2.0 %collective-permute-start.8 = (bf16[128,1024]{1,0:T(8,128)(2,1)}, bf16[128,1024]{1,0:T(8,128)(2,1)S(1)}, u32[]{:S(2)}, u32[]{:S(2)}) collective-permute-start(bf16[128,1024]{1,0:T(8,128)(2,1)} %get-tuple-element.72), channel_id=1, source_target_pairs={{0,6},{2,4},{4,2},{6,0},{8,14},{10,12},{12,10},{14,8},{1,7},{3,5},... | collective-permute-start | bytes 786440 | tf_op jit(solution)/shard_map/ppermute | solution.py:442
  70.3 3.8 %collective-permute-done.10.refs_7_ = bf16[128,1024]{1,0:T(8,128)(2,1)} collective-permute-done((bf16[128,1024]{1,0:T(8,128)(2,1)}, bf16[128,1024]{1,0:T(8,128)(2,1)}, u32[]{:S(2)}, u32[]{:S(2)}) %collective-permute-start.10) | collective-permute-done | bytes 262176 | tf_op jit(solution)/shard_map/ppermute | solution.py:442
  74.1 0.9 copy-done.1
  75.1 10.0 %first_experts.1 = (bf16[128,1024]{1,0:T(8,128)(2,1)S(1)}, bf16[128,1024]{1,0:T(8,128)(2,1)S(1)}, bf16[128,1024]{1,0:T(8,128)(2,1)S(1)}, bf16[128,1024]{1,0:T(8,...) custom-call(s32[1]{0:T(128)} %bitcast.3.core_ref, ...), custom_call_target="tpu_custom_call" | custom-call | flops 1048576 | bytes 1048576 | tf_op jit(solution)/shard_map/first_experts/pallas_call | solution.py:286
  85.1 1.5 %collective-permute-start.11 = (bf16[128,1024]{1,0:T(8,128)(2,1)S(1)}, bf16[128,1024]{1,0:T(8,128)(2,1)S(1)}, u32[]{:S(2)}, u32[]{:S(2)}) collective-permute-start(bf16[128,1024]{1,0:T(8,128)(2,1)S(1)} %get-tuple-element.83), channel_id=1, source_target_pairs={{0,2},{2,0},{4,6},{6,4},{8,10},{10,8},{12,14},{14,12},{1,3},{3,1},... | collective-permute-start | bytes 786440 | tf_op jit(solution)/shard_map/ppermute | solution.py:442
  86.6 2.0 %collective-permute-start.13 = (bf16[128,1024]{1,0:T(8,128)(2,1)S(1)}, bf16[128,1024]{1,0:T(8,128)(2,1)S(1)}, u32[]{:S(2)}, u32[]{:S(2)}) collective-permute-start(bf16[128,1024]{1,0:T(8,128)(2,1)S(1)} %get-tuple-element.85), channel_id=1, source_target_pairs={{0,6},{2,4},{4,2},{6,0},{8,14},{10,12},{12,10},{14,8},{1,7},{3,5},... | collective-permute-start | bytes 786440 | tf_op jit(solution)/shard_map/ppermute | solution.py:442
  88.6 9.4 %last_experts.1 = (bf16[80,1024]{1,0:T(8,128)(2,1)S(1)}, bf16[80,1024]{1,0:T(8,128)(2,1)S(1)}, bf16[80,1024]{1,0:T(8,128)(2,1)S(1)}, bf16[80,1024]{1,0:T(8,128)(...) custom-call(s32[1]{0:T(128)} %bitcast.3.core_ref, ...), custom_call_target="tpu_custom_call", output_to_operand_aliasing={{8}: (12, {}), {9}: (13, {})} | custom-call | flops 1048576 | bytes 1048576 | tf_op jit(solution)/shard_map/last_experts/pallas_call | solution.py:286
  98.1 1.5 %collective-permute-start.14 = (bf16[80,1024]{1,0:T(8,128)(2,1)S(1)}, bf16[80,1024]{1,0:T(8,128)(2,1)S(1)}, u32[]{:S(2)}, u32[]{:S(2)}) collective-permute-start(bf16[80,1024]{1,0:T(8,128)(2,1)S(1)} %get-tuple-element.87), channel_id=1, source_target_pairs={{0,2},{2,0},{4,6},{6,4},{8,10},{10,8},{12,14},{14,12},{1,3},{3,1},... | collective-permute-start | bytes 491528 | tf_op jit(solution)/shard_map/ppermute | solution.py:442
  99.6 0.0 collective-permute-start.15
  99.6 2.0 %collective-permute-start.16 = (bf16[80,1024]{1,0:T(8,128)(2,1)S(1)}, bf16[80,1024]{1,0:T(8,128)(2,1)S(1)}, u32[]{:S(2)}, u32[]{:S(2)}) collective-permute-start(bf16[80,1024]{1,0:T(8,128)(2,1)S(1)} %get-tuple-element.89), channel_id=1, source_target_pairs={{0,6},{2,4},{4,2},{6,0},{8,14},{10,12},{12,10},{14,8},{1,7},{3,5},... | collective-permute-start | bytes 491528 | tf_op jit(solution)/shard_map/ppermute | solution.py:442
  101.6 1.8 %collective-permute-done.14.refs_5_ = bf16[80,1024]{1,0:T(8,128)(2,1)S(1)} collective-permute-done((bf16[80,1024]{1,0:T(8,128)(2,1)S(1)}, bf16[80,1024]{1,0:T(8,128)(2,1)S(1)}, u32[]{:S(2)}, u32[]{:S(2)}) %collective-permute-start.14) | collective-permute-done | bytes 163872 | tf_op jit(solution)/shard_map/ppermute | solution.py:442
  103.5 1.5 %collective-permute-done.15.refs_6_ = bf16[80,1024]{1,0:T(8,128)(2,1)S(1)} collective-permute-done((bf16[80,1024]{1,0:T(8,128)(2,1)S(1)}, bf16[80,1024]{1,0:T(8,128)(2,1)S(1)}, u32[]{:S(2)}, u32[]{:S(2)}) %collective-permute-start.15) | collective-permute-done | bytes 163872 | tf_op jit(solution)/shard_map/ppermute | solution.py:442
  104.9 1.7 %collective-permute-done.16.refs_7_ = bf16[80,1024]{1,0:T(8,128)(2,1)S(1)} collective-permute-done((bf16[80,1024]{1,0:T(8,128)(2,1)S(1)}, bf16[80,1024]{1,0:T(8,128)(2,1)S(1)}, u32[]{:S(2)}, u32[]{:S(2)}) %collective-permute-start.16) | collective-permute-done | bytes 163872 | tf_op jit(solution)/shard_map/ppermute | solution.py:442
  106.7 1.3 relay_sum.1
  108.0 0.1 collective-permute-start.17
  108.0 2.2 %collective-permute-start.21 = (bf16[272,1024]{1,0:T(8,128)(2,1)S(1)}, bf16[272,1024]{1,0:T(8,128)(2,1)S(1)}, u32[]{:S(2)}, u32[]{:S(2)}) collective-permute-start(bf16[272,1024]{1,0:T(8,128)(2,1)S(1)} %relay_sum.1), channel_id=1, source_target_pairs={{0,8},{2,10},{4,12},{6,14},{8,0},{10,2},{12,4},{14,6},{1,9},{3,11}... | collective-permute-start | bytes 1671176 | tf_op jit(solution)/shard_map/ppermute | solution.py:442
  110.2 0.3 collective-permute-start.18
  110.5 2.0 %collective-permute-start.19 = (bf16[80,1024]{1,0:T(8,128)(2,1)S(1)}, bf16[80,1024]{1,0:T(8,128)(2,1)S(1)}, u32[]{:S(2)}, u32[]{:S(2)}) collective-permute-start(bf16[80,1024]{1,0:T(8,128)(2,1)S(1)} %get-tuple-element.100), channel_id=1, source_target_pairs={{0,4},{2,6},{4,0},{6,2},{8,12},{10,14},{12,8},{14,10},{1,5},{3,7},... | collective-permute-start | bytes 491528 | tf_op jit(solution)/shard_map/ppermute | solution.py:442
  112.5 1.2 collective-permute-start.20
  113.7 4.5 %collective-permute-done.17.other_ref = bf16[8,128,3072]{2,1,0:T(8,128)(2,1)S(1)} collective-permute-done((bf16[8,128,3072]{2,1,0:T(8,128)(2,1)S(1)}, bf16[8,128,3072]{2,1,0:T(8,128)(2,1)S(1)}, u32[]{:S(2)}, u32[]{:S(2)}) %collective-permute-start.17) | collective-permute-done | bytes 6291488 | tf_op jit(solution)/shard_map/ppermute | solution.py:445
  118.2 8.0 %weight_pass.1 = (bf16[8,512,1024]{2,1,0:T(8,128)(2,1)}, bf16[8,512,1024]{2,1,0:T(8,128)(2,1)}) custom-call(bf16[8,128,1024]{2,1,0:T(8,128)(2,1)S(1)} %get-tuple-element.79.mine_ref, bf16[8,128,3072]{2,1,0:T(8,128)(2,1)S(1)} %get-tuple-element.90.pack_ref, bf16[8,128,3072]{2,1,0:T(8,128)(2,1)S(1)} %collective-permute-done.17.other_ref), custom_call_target="tpu_custom_call" | custom-call | flops 1048576 | bytes 1048576 | tf_op jit(solution)/shard_map/weight_pass/pallas_call | solution.py:321
  126.2 0.5 collective-permute-done.19.refs_6_
  126.7 3.1 %collective-permute-done.20.refs_7_ = bf16[80,1024]{1,0:T(8,128)(2,1)S(1)} collective-permute-done((bf16[80,1024]{1,0:T(8,128)(2,1)S(1)}, bf16[80,1024]{1,0:T(8,128)(2,1)S(1)}, u32[]{:S(2)}, u32[]{:S(2)}) %collective-permute-start.20) | collective-permute-done | bytes 163872 | tf_op jit(solution)/shard_map/ppermute | solution.py:442
  129.8 1.3 near_sum.1
  131.1 4.8 %collective-permute-done.21.back_ref = bf16[272,1024]{1,0:T(8,128)(2,1)S(1)} collective-permute-done((bf16[272,1024]{1,0:T(8,128)(2,1)S(1)}, bf16[272,1024]{1,0:T(8,128)(2,1)S(1)}, u32[]{:S(2)}, u32[]{:S(2)}) %collective-permute-start.21) | collective-permute-done | bytes 557088 | tf_op jit(solution)/shard_map/ppermute | solution.py:442
  135.9 1.3 last_sum.1
  (19 shorter events, 0.0 us)
Async XLA Ops:
  1.9 53.0 %collective-permute-start.3 = (bf16[272,1024]{1,0:T(8,128)(2,1)S(1)}, bf16[272,1024]{1,0:T(8,128)(2,1)S(1)}, u32[]{:S(2)}, u32[]{:S(2)}) collective-permute-start(bf16[272,1024]{1,0:T(8,128)(2,1)S(1)} %get-tuple-element.56.g_ref), channel_id=1, source_target_pairs={{0,8},{2,10},{4,12},{6,14},{8,0},{10,2},{12,4},{14,6},{1,9},{3,11}... | collective-permute-start | bytes 1671176 | tf_op jit(solution)/shard_map/ppermute | solution.py:442
  7.0 19.0 %copy-start.2 = (bf16[4,128,256]{2,1,0:T(8,128)(2,1)}, bf16[4,128,256]{2,1,0:T(8,128)(2,1)S(1)}, u32[]{:S(2)}) copy-start(bf16[4,128,256]{2,1,0:T(8,128)(2,1)S(1)} %get-tuple-element.93.select_ref) | copy-start | bytes 786436
  7.0 34.5 %collective-permute-start = (bf16[256,1024]{1,0:T(8,128)(2,1)S(1)}, bf16[256,1024]{1,0:T(8,128)(2,1)S(1)}, u32[]{:S(2)}, u32[]{:S(2)}) collective-permute-start(bf16[256,1024]{1,0:T(8,128)(2,1)S(1)} %get-tuple-element.60), channel_id=1, source_target_pairs={{0,2},{2,0},{4,6},{6,4},{8,10},{10,8},{12,14},{14,12},{1,3},{3,1},... | collective-permute-start | bytes 1572872 | tf_op jit(solution)/shard_map/ppermute | solution.py:442
  8.6 36.9 %collective-permute-start.1 = (bf16[256,1024]{1,0:T(8,128)(2,1)S(1)}, bf16[256,1024]{1,0:T(8,128)(2,1)S(1)}, u32[]{:S(2)}, u32[]{:S(2)}) collective-permute-start(bf16[256,1024]{1,0:T(8,128)(2,1)S(1)} %get-tuple-element.61), channel_id=1, source_target_pairs={{0,4},{2,6},{4,0},{6,2},{8,12},{10,14},{12,8},{14,10},{1,5},{3,7},... | collective-permute-start | bytes 1572872 | tf_op jit(solution)/shard_map/ppermute | solution.py:442
  10.2 44.8 %collective-permute-start.2 = (bf16[256,1024]{1,0:T(8,128)(2,1)S(1)}, bf16[256,1024]{1,0:T(8,128)(2,1)S(1)}, u32[]{:S(2)}, u32[]{:S(2)}) collective-permute-start(bf16[256,1024]{1,0:T(8,128)(2,1)S(1)} %get-tuple-element.62), channel_id=1, source_target_pairs={{0,6},{2,4},{4,2},{6,0},{8,14},{10,12},{12,10},{14,8},{1,7},{3,5},... | collective-permute-start | bytes 1572872 | tf_op jit(solution)/shard_map/ppermute | solution.py:442
  10.6 44.4 %collective-permute-start.4 = (bf16[256,1024]{1,0:T(8,128)(2,1)}, bf16[256,1024]{1,0:T(8,128)(2,1)S(1)}, u32[]{:S(2)}, u32[]{:S(2)}) collective-permute-start(bf16[256,1024]{1,0:T(8,128)(2,1)} %x_hbm.1), channel_id=1, source_target_pairs={{0,8},{2,10},{4,12},{6,14},{8,0},{10,2},{12,4},{14,6},{1,9},{3,11}... | collective-permute-start | bytes 1572872 | tf_op jit(solution)/shard_map/ppermute | solution.py:442
  56.8 0.7 copy-start.4
  57.4 8.6 %collective-permute-start.5 = (bf16[128,1024]{1,0:T(8,128)(2,1)S(1)}, bf16[128,1024]{1,0:T(8,128)(2,1)S(1)}, u32[]{:S(2)}, u32[]{:S(2)}) collective-permute-start(bf16[128,1024]{1,0:T(8,128)(2,1)S(1)} %get-tuple-element.68), channel_id=1, source_target_pairs={{0,2},{2,0},{4,6},{6,4},{8,10},{10,8},{12,14},{14,12},{1,3},{3,1},... | collective-permute-start | bytes 786440 | tf_op jit(solution)/shard_map/ppermute | solution.py:442
  58.9 11.4 %collective-permute-start.9 = (bf16[128,1024]{1,0:T(8,128)(2,1)}, bf16[128,1024]{1,0:T(8,128)(2,1)}, u32[]{:S(2)}, u32[]{:S(2)}) collective-permute-start(bf16[128,1024]{1,0:T(8,128)(2,1)} %get-tuple-element.74), channel_id=1, source_target_pairs={{0,4},{2,6},{4,0},{6,2},{8,12},{10,14},{12,8},{14,10},{1,5},{3,7},... | collective-permute-start | bytes 786440 | tf_op jit(solution)/shard_map/ppermute | solution.py:442
  58.9 15.2 %collective-permute-start.10 = (bf16[128,1024]{1,0:T(8,128)(2,1)}, bf16[128,1024]{1,0:T(8,128)(2,1)}, u32[]{:S(2)}, u32[]{:S(2)}) collective-permute-start(bf16[128,1024]{1,0:T(8,128)(2,1)} %get-tuple-element.75), channel_id=1, source_target_pairs={{0,6},{2,4},{4,2},{6,0},{8,14},{10,12},{12,10},{14,8},{1,7},{3,5},... | collective-permute-start | bytes 786440 | tf_op jit(solution)/shard_map/ppermute | solution.py:442
  66.1 0.7 copy-start
  66.8 19.8 %collective-permute-start.6 = (bf16[128,1024]{1,0:T(8,128)(2,1)}, bf16[128,1024]{1,0:T(8,128)(2,1)S(1)}, u32[]{:S(2)}, u32[]{:S(2)}) collective-permute-start(bf16[128,1024]{1,0:T(8,128)(2,1)} %get-tuple-element.70), channel_id=1, source_target_pairs={{0,2},{2,0},{4,6},{6,4},{8,10},{10,8},{12,14},{14,12},{1,3},{3,1},... | collective-permute-start | bytes 786440 | tf_op jit(solution)/shard_map/ppermute | solution.py:442
  68.2 20.4 %collective-permute-start.7 = (bf16[128,1024]{1,0:T(8,128)(2,1)}, bf16[128,1024]{1,0:T(8,128)(2,1)S(1)}, u32[]{:S(2)}, u32[]{:S(2)}) collective-permute-start(bf16[128,1024]{1,0:T(8,128)(2,1)} %get-tuple-element.71), channel_id=1, source_target_pairs={{0,4},{2,6},{4,0},{6,2},{8,12},{10,14},{12,8},{14,10},{1,5},{3,7},... | collective-permute-start | bytes 786440 | tf_op jit(solution)/shard_map/ppermute | solution.py:442
  68.2 20.4 %collective-permute-start.8 = (bf16[128,1024]{1,0:T(8,128)(2,1)}, bf16[128,1024]{1,0:T(8,128)(2,1)S(1)}, u32[]{:S(2)}, u32[]{:S(2)}) collective-permute-start(bf16[128,1024]{1,0:T(8,128)(2,1)} %get-tuple-element.72), channel_id=1, source_target_pairs={{0,6},{2,4},{4,2},{6,0},{8,14},{10,12},{12,10},{14,8},{1,7},{3,5},... | collective-permute-start | bytes 786440 | tf_op jit(solution)/shard_map/ppermute | solution.py:442
  74.1 1.0 copy-start.1
  85.1 14.6 %collective-permute-start.11 = (bf16[128,1024]{1,0:T(8,128)(2,1)S(1)}, bf16[128,1024]{1,0:T(8,128)(2,1)S(1)}, u32[]{:S(2)}, u32[]{:S(2)}) collective-permute-start(bf16[128,1024]{1,0:T(8,128)(2,1)S(1)} %get-tuple-element.83), channel_id=1, source_target_pairs={{0,2},{2,0},{4,6},{6,4},{8,10},{10,8},{12,14},{14,12},{1,3},{3,1},... | collective-permute-start | bytes 786440 | tf_op jit(solution)/shard_map/ppermute | solution.py:442
  86.6 15.0 %collective-permute-start.12 = (bf16[128,1024]{1,0:T(8,128)(2,1)S(1)}, bf16[128,1024]{1,0:T(8,128)(2,1)S(1)}, u32[]{:S(2)}, u32[]{:S(2)}) collective-permute-start(bf16[128,1024]{1,0:T(8,128)(2,1)S(1)} %get-tuple-element.84), channel_id=1, source_target_pairs={{0,4},{2,6},{4,0},{6,2},{8,12},{10,14},{12,8},{14,10},{1,5},{3,7},... | collective-permute-start | bytes 786440 | tf_op jit(solution)/shard_map/ppermute | solution.py:442
  86.6 15.0 %collective-permute-start.13 = (bf16[128,1024]{1,0:T(8,128)(2,1)S(1)}, bf16[128,1024]{1,0:T(8,128)(2,1)S(1)}, u32[]{:S(2)}, u32[]{:S(2)}) collective-permute-start(bf16[128,1024]{1,0:T(8,128)(2,1)S(1)} %get-tuple-element.85), channel_id=1, source_target_pairs={{0,6},{2,4},{4,2},{6,0},{8,14},{10,12},{12,10},{14,8},{1,7},{3,5},... | collective-permute-start | bytes 786440 | tf_op jit(solution)/shard_map/ppermute | solution.py:442
  88.6 18.0 %copy-start.5 = (bf16[4,128,256]{2,1,0:T(8,128)(2,1)S(1)}, bf16[4,128,256]{2,1,0:T(8,128)(2,1)}, u32[]{:S(2)}) copy-start(bf16[4,128,256]{2,1,0:T(8,128)(2,1)} %copy-done.4) | copy-start | bytes 786436
  98.1 5.4 %collective-permute-start.14 = (bf16[80,1024]{1,0:T(8,128)(2,1)S(1)}, bf16[80,1024]{1,0:T(8,128)(2,1)S(1)}, u32[]{:S(2)}, u32[]{:S(2)}) collective-permute-start(bf16[80,1024]{1,0:T(8,128)(2,1)S(1)} %get-tuple-element.87), channel_id=1, source_target_pairs={{0,2},{2,0},{4,6},{6,4},{8,10},{10,8},{12,14},{14,12},{1,3},{3,1},... | collective-permute-start | bytes 491528 | tf_op jit(solution)/shard_map/ppermute | solution.py:442
  99.6 5.3 %collective-permute-start.15 = (bf16[80,1024]{1,0:T(8,128)(2,1)S(1)}, bf16[80,1024]{1,0:T(8,128)(2,1)S(1)}, u32[]{:S(2)}, u32[]{:S(2)}) collective-permute-start(bf16[80,1024]{1,0:T(8,128)(2,1)S(1)} %get-tuple-element.88), channel_id=1, source_target_pairs={{0,4},{2,6},{4,0},{6,2},{8,12},{10,14},{12,8},{14,10},{1,5},{3,7},... | collective-permute-start | bytes 491528 | tf_op jit(solution)/shard_map/ppermute | solution.py:442
  99.6 7.0 %collective-permute-start.16 = (bf16[80,1024]{1,0:T(8,128)(2,1)S(1)}, bf16[80,1024]{1,0:T(8,128)(2,1)S(1)}, u32[]{:S(2)}, u32[]{:S(2)}) collective-permute-start(bf16[80,1024]{1,0:T(8,128)(2,1)S(1)} %get-tuple-element.89), channel_id=1, source_target_pairs={{0,6},{2,4},{4,2},{6,0},{8,14},{10,12},{12,10},{14,8},{1,7},{3,5},... | collective-permute-start | bytes 491528 | tf_op jit(solution)/shard_map/ppermute | solution.py:442
  106.7 23.1 %copy-start.3 = (bf16[4,128,256]{2,1,0:T(8,128)(2,1)S(1)}, bf16[4,128,256]{2,1,0:T(8,128)(2,1)}, u32[]{:S(2)}) copy-start(bf16[4,128,256]{2,1,0:T(8,128)(2,1)} %copy-done.2) | copy-start | bytes 786436
  108.0 10.2 %collective-permute-start.17 = (bf16[8,128,3072]{2,1,0:T(8,128)(2,1)S(1)}, bf16[8,128,3072]{2,1,0:T(8,128)(2,1)S(1)}, u32[]{:S(2)}, u32[]{:S(2)}) collective-permute-start(bf16[8,128,3072]{2,1,0:T(8,128)(2,1)S(1)} %get-tuple-element.90.pack_ref), channel_id=1, source_target_pairs={{0,1},{1,0},{2,3},{3,2},{4,5},{5,4},{6,7},{7,6},{8,9},{9,8},{10,11... | collective-permute-start | bytes 18874376 | tf_op jit(solution)/shard_map/ppermute | solution.py:445
  108.0 27.9 %collective-permute-start.21 = (bf16[272,1024]{1,0:T(8,128)(2,1)S(1)}, bf16[272,1024]{1,0:T(8,128)(2,1)S(1)}, u32[]{:S(2)}, u32[]{:S(2)}) collective-permute-start(bf16[272,1024]{1,0:T(8,128)(2,1)S(1)} %relay_sum.1), channel_id=1, source_target_pairs={{0,8},{2,10},{4,12},{6,14},{8,0},{10,2},{12,4},{14,6},{1,9},{3,11}... | collective-permute-start | bytes 1671176 | tf_op jit(solution)/shard_map/ppermute | solution.py:442
  110.2 16.0 %collective-permute-start.18 = (bf16[80,1024]{1,0:T(8,128)(2,1)S(1)}, bf16[80,1024]{1,0:T(8,128)(2,1)S(1)}, u32[]{:S(2)}, u32[]{:S(2)}) collective-permute-start(bf16[80,1024]{1,0:T(8,128)(2,1)S(1)} %get-tuple-element.99), channel_id=1, source_target_pairs={{0,2},{2,0},{4,6},{6,4},{8,10},{10,8},{12,14},{14,12},{1,3},{3,1},... | collective-permute-start | bytes 491528 | tf_op jit(solution)/shard_map/ppermute | solution.py:442
  110.5 16.2 %collective-permute-start.19 = (bf16[80,1024]{1,0:T(8,128)(2,1)S(1)}, bf16[80,1024]{1,0:T(8,128)(2,1)S(1)}, u32[]{:S(2)}, u32[]{:S(2)}) collective-permute-start(bf16[80,1024]{1,0:T(8,128)(2,1)S(1)} %get-tuple-element.100), channel_id=1, source_target_pairs={{0,4},{2,6},{4,0},{6,2},{8,12},{10,14},{12,8},{14,10},{1,5},{3,7},... | collective-permute-start | bytes 491528 | tf_op jit(solution)/shard_map/ppermute | solution.py:442
  112.5 17.3 %collective-permute-start.20 = (bf16[80,1024]{1,0:T(8,128)(2,1)S(1)}, bf16[80,1024]{1,0:T(8,128)(2,1)S(1)}, u32[]{:S(2)}, u32[]{:S(2)}) collective-permute-start(bf16[80,1024]{1,0:T(8,128)(2,1)S(1)} %get-tuple-element.101), channel_id=1, source_target_pairs={{0,6},{2,4},{4,2},{6,0},{8,14},{10,12},{12,10},{14,8},{1,7},{3,5},... | collective-permute-start | bytes 491528 | tf_op jit(solution)/shard_map/ppermute | solution.py:442

commit v2 on v1

--- a/solution.py
+++ b/solution.py
@@ -9,6 +9,7 @@
 
 EXPERTS = 64
 CAP = 16
+EIGHTHS = 3
 BF = jnp.bfloat16
 F32 = jnp.float32
 NT = (((1,), (1,)), ((), ()))
@@ -120,18 +121,17 @@
     return pl.BlockSpec(shape, lambda j: (j,) + (0,) * (len(shape) - 1))
 
 
-def rows_kernel(peers, parts, me_ref, g_ref, x_ref, select_ref, facts_ref, *rows_refs):
-    slots, tokens = select_ref.shape[1:]
-    size = slots // parts
+def rows_kernel(peers, sizes, me_ref, g_ref, x_ref, facts_ref, *rows_refs):
+    tokens, slots = x_ref.shape[0], sum(sizes)
     tgt, gates = facts_of(g_ref, tokens)
     for m in range(peers):
         select, gate = select_slots(tgt, gates, (me_ref[0] ^ m) * slots, slots)
-        select_ref[m] = select
         x = dot(select, x_ref[...], NN).astype(BF)
         d = (gate * dot(select, g_ref[0:tokens], NN)).astype(BF)
-        for i in range(parts):
-            rows_refs[i * peers + m][0:size] = x[i * size : (i + 1) * size]
-            rows_refs[i * peers + m][size:] = d[i * size : (i + 1) * size]
+        for i, size in enumerate(sizes):
+            at = slice(sum(sizes[:i]), sum(sizes[:i]) + size)
+            rows_refs[i * peers + m][0:size] = x[at]
+            rows_refs[i * peers + m][size:] = d[at]
     facts_ref[0:2] = jnp.concatenate(tgt, axis=0).astype(F32)
     facts_ref[2:4] = jnp.concatenate(gates, axis=0)
     facts_ref[4:8] = jnp.zeros((4, tokens), F32)
@@ -141,19 +141,19 @@
 VECTORS = pl.BlockSpec(memory_space=pltpu.VMEM)
 
 
-def rows_pass(name, parts, me, g, x, peers, slots):
+def rows_pass(name, sizes, me, g, x, peers):
     tokens, width = x.shape
     out = pl.pallas_call(
-        functools.partial(rows_kernel, peers, parts),
-        out_shape=[jax.ShapeDtypeStruct((peers, slots, tokens), BF), jax.ShapeDtypeStruct((8, tokens), F32)]
-        + [jax.ShapeDtypeStruct((2 * slots // parts, width), BF)] * (parts * peers),
+        functools.partial(rows_kernel, peers, sizes),
+        out_shape=[jax.ShapeDtypeStruct((8, tokens), F32)]
+        + [jax.ShapeDtypeStruct((2 * size, width), BF) for size in sizes for _ in range(peers)],
         in_specs=[SCALARS] + [VECTORS] * 2,
-        out_specs=[VECTORS] * (2 + parts * peers),
+        out_specs=[VECTORS] * (1 + len(sizes) * peers),
         compiler_params=params(),
         cost_estimate=COST,
         name=name,
     )(me, g, x)
-    return out[0], out[1], *(list(out[2 + i * peers : 2 + (i + 1) * peers]) for i in range(parts))
+    return out[0], *(list(out[1 + i * peers : 1 + (i + 1) * peers]) for i in range(len(sizes)))
 
 
 def fetch(weight_hbm, weight_ref, sem, first=0):
@@ -206,23 +206,25 @@
     pack_ref, mine_ref, in_sem, out_sem = refs
     experts = up_ref.shape[0]
     width = far_refs[0].shape[1]
-    slots, half, count = experts * CAP, mine_ref.shape[2] // 2, 2 * peers * CAP
+    slots, half = experts * CAP, mine_ref.shape[2] // 2
+    all_slots = near_refs[0].shape[0] // 2
+    start = up_hbm.shape[0] - experts if which else 0
     core = core_ref[0]
 
     def store(j):
         return (
-            pltpu.make_async_copy(pack_ref.at[j], pack_hbm.at[which * experts + j], out_sem.at[j, 0]),
-            pltpu.make_async_copy(mine_ref.at[j], mine_hbm.at[which * experts + j], out_sem.at[j, 1]),
+            pltpu.make_async_copy(pack_ref.at[j], pack_hbm.at[start + j], out_sem.at[j, 0]),
+            pltpu.make_async_copy(mine_ref.at[j], mine_hbm.at[start + j], out_sem.at[j, 1]),
         )
 
     def rows_of(j, kind):
-        near, far = (2 * kind + which) * slots + j * CAP, kind * slots + j * CAP
+        near, far = kind * all_slots + (start + j) * CAP, kind * slots + j * CAP
         return joined([ref[near : near + CAP] for ref in near_refs] + [ref[far : far + CAP] for ref in far_refs])
 
     weights = ((up_hbm, up_ref), (down_hbm, down_ref))
     copies = [
         [
-            pltpu.make_async_copy(hbm.at[which * experts + j], ref.at[j], in_sem.at[j, i])
+            pltpu.make_async_copy(hbm.at[start + j], ref.at[j], in_sem.at[j, i])
             for i, (hbm, ref) in enumerate(weights)
         ]
         for j in range(experts)
@@ -269,15 +271,21 @@
     if which:
         for m in range(2 * peers):
             total = jnp.sum(joined([early_part[0][m], part_ref[m]]).T, axis=0, keepdims=True)
-            gx_refs[m][slots:, 0 : 2 * slots] = joined([*thirds(total), jnp.zeros((CAP - 3, 2 * slots), BF)])
-            gx_refs[m][slots:, 2 * slots :] = jnp.zeros((CAP, width - 2 * slots), BF)
+            gx_refs[m][slots:, 0:all_slots] = joined([*thirds(total), jnp.zeros((CAP - 3, all_slots), BF)])
+            gx_refs[m][slots:, all_slots:] = jnp.zeros((CAP, width - all_slots), BF)
     for j in range(experts):
         for out in store(j):
             out.wait()
 
 
+def first_share(experts):
+    return max(1, experts * EIGHTHS // 8)
+
+
 def block_pass(which, core, up, down, near, far, early=()):
-    experts, width, hidden = up.shape[0] // 2, *up.shape[1:]
+    all_experts, width, hidden = up.shape
+    experts = first_share(all_experts)
+    experts = all_experts - experts if which else experts
     peers = len(near)
     count, slots = 2 * peers * CAP, experts * CAP
     pack, mine, part = (experts, count, 2 * width + hidden), (experts, count, hidden), (2 * peers, slots, 128)
@@ -287,7 +295,7 @@
         functools.partial(block_kernel, peers, which),
         out_shape=[jax.ShapeDtypeStruct(shape, BF) for shape in gx]
         + ([] if which else [jax.ShapeDtypeStruct(part, F32)])
-        + [jax.ShapeDtypeStruct((2 * experts, *shape[1:]), BF) for shape in (pack, mine)],
+        + [jax.ShapeDtypeStruct((all_experts, *shape[1:]), BF) for shape in (pack, mine)],
         in_specs=[SCALARS] + [IN_HBM] * 2 + [VECTORS] * (2 * peers + which) + [anywhere] * (2 * which),
         out_specs=[VECTORS] * (len(gx) + 1 - which) + [anywhere] * 2,
         scratch_shapes=[pltpu.VMEM((experts, width, hidden), BF)] * 2
@@ -299,7 +307,7 @@
             pltpu.SemaphoreType.DMA((experts, 2)),
         ],
         input_output_aliases={4 + 2 * peers + i: len(gx) + i for i in range(2 * which)},
-        compiler_params=params(26),
+        compiler_params=params(6 * experts + 4),
         cost_estimate=COST,
         name=("first_experts", "last_experts")[which],
     )(core, in_hbm(up), in_hbm(down), *near, *far, *early)
@@ -330,36 +338,46 @@
     )(mine, pack, other)
 
 
+def targets_in(facts_ref):
+    return facts_ref[0:1, :].astype(jnp.int32), facts_ref[1:2, :].astype(jnp.int32)
+
+
+def selection(tgt, base, slots):
+    rows = lax.broadcasted_iota(jnp.int32, (slots, tgt[0].shape[1]), 0) + base
+    return jnp.where((rows == tgt[0]) | (rows == tgt[1]), 1.0, 0.0).astype(BF)
+
+
 def tail_rows(peers):
     return -(-3 * peers // CAP) * CAP
 
 
-def relay_kernel(peers, select_ref, *refs):
+def relay_kernel(peers, me_ref, facts_ref, *refs):
     early_refs, late_refs, out_ref = refs[:peers], refs[peers : 2 * peers], refs[2 * peers]
-    slots, tokens = select_ref.shape[1:]
-    half, width = slots // 2, out_ref.shape[1]
+    tokens, width = facts_ref.shape[1], out_ref.shape[1]
+    half, rest = early_refs[0].shape[0] // 2, late_refs[0].shape[0] - CAP
+    slots = half + rest
+    tgt = targets_in(facts_ref)
     total = None
     for m in range(peers):
-        term = dot(select_ref[m, 0:half], early_refs[m][half:], TN) + dot(
-            select_ref[m, half:], late_refs[m][0:half], TN
-        )
+        rows = joined([early_refs[m][half:], late_refs[m][0:rest]])
+        term = dot(selection(tgt, (me_ref[0] ^ m) * slots, slots), rows, TN)
         total = term if total is None else total + term
     out_ref[0:tokens] = total.astype(BF)
-    tails = [ref[half : half + 3] for ref in late_refs]
+    tails = [ref[rest : rest + 3] for ref in late_refs]
     out_ref[tokens:] = joined([*tails, jnp.zeros((tail_rows(peers) - 3 * peers, width), BF)])
 
 
-def relay_pass(select, early, late):
-    peers, slots, tokens = select.shape
+def relay_pass(me, facts, early, late):
+    peers, tokens = len(early), facts.shape[1]
     return pl.pallas_call(
         functools.partial(relay_kernel, peers),
         out_shape=jax.ShapeDtypeStruct((tokens + tail_rows(peers), early[0].shape[1]), BF),
-        in_specs=[VECTORS] * (1 + 2 * peers),
+        in_specs=[SCALARS] + [VECTORS] * (1 + 2 * peers),
         out_specs=VECTORS,
         compiler_params=params(),
         cost_estimate=COST,
         name="relay_sum",
-    )(select, *early, *late)
+    )(me, facts, *early, *late)
 
 
 def slot_values(tgt, chip, tail, slots):
@@ -368,38 +386,34 @@
     return [jnp.sum(jnp.where(at == t, column, 0.0), axis=0, keepdims=True) for t in tgt]
 
 
-def targets_in(facts_ref):
-    return facts_ref[0:1, :].astype(jnp.int32), facts_ref[1:2, :].astype(jnp.int32)
-
-
-def near_sum_kernel(me_ref, facts_ref, select_ref, *refs):
-    peers, slots, tokens = select_ref.shape
+def near_sum_kernel(peers, me_ref, facts_ref, *refs):
     early_refs, late_refs, (out_ref, gates_ref) = refs[:peers], refs[peers : 2 * peers], refs[2 * peers :]
-    half = slots // 2
+    tokens = facts_ref.shape[1]
+    half, rest = early_refs[0].shape[0] // 2, late_refs[0].shape[0] - CAP
+    slots = half + rest
     tgt = targets_in(facts_ref)
     total, values = None, [jnp.zeros((1, tokens), F32)] * 2
     for m in range(peers):
-        term = dot(select_ref[m, 0:half], early_refs[m][0:half], TN) + dot(
-            select_ref[m, half:], late_refs[m][0:half], TN
-        )
+        rows = joined([early_refs[m][0:half], late_refs[m][0:rest]])
+        term = dot(selection(tgt, (me_ref[0] ^ m) * slots, slots), rows, TN)
         total = term if total is None else total + term
-        more = slot_values(tgt, me_ref[0] ^ m, late_refs[m][half : half + CAP, 0:slots], slots)
+        more = slot_values(tgt, me_ref[0] ^ m, late_refs[m][rest : rest + CAP, 0:slots], slots)
         values = [value + new for value, new in zip(values, more)]
     out_ref[...] = total.astype(BF)
     gates_ref[...] = joined(values)
 
 
-def near_sum(me, facts, select, early, late):
-    tokens, width = select.shape[2], early[0].shape[1]
+def near_sum(me, facts, early, late):
+    tokens, width = facts.shape[1], early[0].shape[1]
     return pl.pallas_call(
-        near_sum_kernel,
+        functools.partial(near_sum_kernel, len(early)),
         out_shape=[jax.ShapeDtypeStruct((tokens, width), BF), jax.ShapeDtypeStruct((2, tokens), F32)],
-        in_specs=[SCALARS] + [VECTORS] * (2 + 2 * len(early)),
+        in_specs=[SCALARS] + [VECTORS] * (1 + 2 * len(early)),
         out_specs=[VECTORS] * 2,
         compiler_params=params(),
         cost_estimate=COST,
         name="near_sum",
-    )(me, facts, select, *early, *late)
+    )(me, facts, *early, *late)
 
 
 def last_kernel(peers, me_ref, facts_ref, near_ref, values_ref, back_ref, out_ref, gates_ref):
@@ -434,7 +448,7 @@
 def per_device(tokens, routes, gate_values, up_weight, down_weight, grad_out):
     chips = lax.axis_size("expert")
     half = chips // 2
-    slots = up_weight.shape[0] * CAP
+    slots, first = up_weight.shape[0] * CAP, first_share(up_weight.shape[0]) * CAP
     me = lax.axis_index("expert").astype(jnp.int32).reshape(1)
     core = lax.axis_index("dp").astype(jnp.int32).reshape(1)
 
@@ -450,11 +464,11 @@
     g_near, x_near = prepare(routes.T, gate_values.T, grad_out, tokens)
     g_far = swap(g_near, half)
     x_far = swap(tokens, half)
-    select, facts, near = rows_pass("near_rows", 1, me, g_near, x_near, half, slots)
+    facts, near = rows_pass("near_rows", (slots,), me, g_near, x_near, half)
     near = deal(near)
     weights = turned(up_weight), turned(down_weight)
-    select_far, _, far_first, far_last = rows_pass(
-        "far_rows", 2, me, after(g_far, near, weights), x_far, half, slots
+    facts_far, far_first, far_last = rows_pass(
+        "far_rows", (first, slots - first), me, after(g_far, near, weights), x_far, half
     )
     far_first = deal(far_first)
     far_last = deal(after(far_last, far_first[1]))
@@ -462,13 +476,13 @@
     gx_first, part, pack, mine = block_pass(0, core, *weights, near, far_first)
     gx_first = deal(gx_first)
     gx_last, pack, mine = block_pass(1, core, *weights, near, far_last, (part, pack, mine))
-    relay = relay_pass(select_far, gx_first, deal(gx_last[half:]))
+    relay = relay_pass(me, facts_far, gx_first, deal(gx_last[half:]))
     back = swap(relay, half)
     other = swap_core(after(pack, relay))
     near_last = deal(after(gx_last[:half], relay))
 
     grad_up, grad_down = weight_pass(mine, pack, other)
-    near_tokens, near_gates = near_sum(me, after(facts, grad_up), select, gx_first, near_last)
+    near_tokens, near_gates = near_sum(me, after(facts, grad_up), gx_first, near_last)
     grad_tokens, grad_gates = last_pass(half, me, facts, near_tokens, near_gates, after(back, near_tokens))
     return grad_tokens, grad_gates.T, grad_up, grad_down
 

time: 138 us -> 136 us (0.986)
  waiting for transfers between devices: 40.3 us -> 38.8 us
    ppermute x21, waiting for transfers between devices: 35.8 us -> 33.8 us  [swap(): return lax.ppermute(value, 'expert', [(i, i ^ m) for i in range(chips)])]
    unnamed x12 -> x8, local copies, waits for them, and re-layouts: 2.36 us -> 3.2 us
  transfers between devices with their start and end apart: 22 -> 22, of which waited for: 11 -> 12; matrix products, arithmetic and copies ran while one was open for 0% -> 0% of each run, Pallas kernels for 44% -> 45%
where the time goes in v2:
time: 136 us
  Pallas kernels  66.3 us (49%)
  waiting for transfers between devices  38.8 us (29%)
  starting transfers between devices  26.9 us (20%)
  local copies, waits for them, and re-layouts  3.2 us (2%)
    ppermute x21, waiting for transfers between devices, swap(): return lax.ppermute(value, 'expert', [(i, i ^ m) for i in range(chips)])  33.8 us
    pallas_call x2, Pallas kernels, turned(): pl.pallas_call(turn_kernel, grid=(experts,), out_shape=pltpu.HBM((experts...  30.9 us
    ppermute x21, starting transfers between devices, swap(): return lax.ppermute(value, 'expert', [(i, i ^ m) for i in range(chips)])  26.8 us
    pallas_call x2, Pallas kernels, block_pass(): pl.pallas_call(functools.partial(block_kernel, peers, which), out_shape=[...  20.2 us
    pallas_call x1, Pallas kernels, weight_pass(): pl.pallas_call(weight_kernel, grid=(experts,), out_shape=[jax.ShapeDtypeS...  8.04 us
    ppermute x1, waiting for transfers between devices, swap_core(): return lax.ppermute(value, 'dp', [(0, 1), (1, 0)])  5.07 us
    unnamed x8, local copies, waits for them, and re-layouts  3.2 us
    pallas_call x2, Pallas kernels, rows_pass(): pl.pallas_call(functools.partial(rows_kernel, peers, sizes), out_shape=[j...  2.9 us
  transfers between devices with their start and end apart: 22, of which 12 were waited for; matrix products, arithmetic and copies ran while one was open for 0% of the time, Pallas kernels for 45%

profile of v2, /device:TPU:0, one launch (start us, length us, event | category | flops | bytes accessed | tf_op | source)
XLA Modules:
  0.0 135.9 jit_solution(16155079830402246762)
XLA Ops:
  0.6 1.3 prepare.1
  1.9 4.1 %collective-permute-start.3 = (bf16[272,1024]{1,0:T(8,128)(2,1)S(1)}, bf16[272,1024]{1,0:T(8,128)(2,1)S(1)}, u32[]{:S(2)}, u32[]{:S(2)}) collective-permute-start(bf16[272,1024]{1,0:T(8,128)(2,1)S(1)} %get-tuple-element.55.g_ref), channel_id=1, source_target_pairs={{0,8},{2,10},{4,12},{6,14},{8,0},{10,2},{12,4},{14,6},{1,9},{3,11}... | collective-permute-start | bytes 1671176 | tf_op jit(solution)/shard_map/ppermute | solution.py:456
  6.0 1.0 near_rows.1
  7.0 1.6 %collective-permute-start = (bf16[256,1024]{1,0:T(8,128)(2,1)S(1)}, bf16[256,1024]{1,0:T(8,128)(2,1)S(1)}, u32[]{:S(2)}, u32[]{:S(2)}) collective-permute-start(bf16[256,1024]{1,0:T(8,128)(2,1)S(1)} %get-tuple-element.59), channel_id=1, source_target_pairs={{0,2},{2,0},{4,6},{6,4},{8,10},{10,8},{12,14},{14,12},{1,3},{3,1},... | collective-permute-start | bytes 1572872 | tf_op jit(solution)/shard_map/ppermute | solution.py:456
  8.6 1.6 %collective-permute-start.1 = (bf16[256,1024]{1,0:T(8,128)(2,1)S(1)}, bf16[256,1024]{1,0:T(8,128)(2,1)S(1)}, u32[]{:S(2)}, u32[]{:S(2)}) collective-permute-start(bf16[256,1024]{1,0:T(8,128)(2,1)S(1)} %get-tuple-element.60), channel_id=1, source_target_pairs={{0,4},{2,6},{4,0},{6,2},{8,12},{10,14},{12,8},{14,10},{1,5},{3,7},... | collective-permute-start | bytes 1572872 | tf_op jit(solution)/shard_map/ppermute | solution.py:456
  10.2 0.4 collective-permute-start.2
  10.6 0.0 collective-permute-start.4
  10.6 15.5 %turned.2.up_hbm = bf16[8,1024,1024]{2,1,0:T(8,128)(2,1)} custom-call(bf16[8,1024,1024]{2,1,0:T(8,128)(2,1)} %weight_ref.2), custom_call_target="tpu_custom_call" | custom-call | flops 1048576 | bytes 1048576 | tf_op jit(solution)/shard_map/turned/pallas_call | solution.py:175
  26.1 15.5 %turned.3.down_hbm = bf16[8,1024,1024]{2,1,0:T(8,128)(2,1)} custom-call(bf16[8,1024,1024]{2,1,0:T(8,128)(2,1)} %weight_ref.3), custom_call_target="tpu_custom_call" | custom-call | flops 1048576 | bytes 1048576 | tf_op jit(solution)/shard_map/turned/pallas_call | solution.py:175
  41.5 0.0 collective-permute-done.refs_1_
  41.5 3.9 %collective-permute-done.1.refs_2_ = bf16[256,1024]{1,0:T(8,128)(2,1)S(1)} collective-permute-done((bf16[256,1024]{1,0:T(8,128)(2,1)S(1)}, bf16[256,1024]{1,0:T(8,128)(2,1)S(1)}, u32[]{:S(2)}, u32[]{:S(2)}) %collective-permute-start.1) | collective-permute-done | bytes 524320 | tf_op jit(solution)/shard_map/ppermute | solution.py:456
  45.5 9.5 %collective-permute-done.2.refs_3_ = bf16[256,1024]{1,0:T(8,128)(2,1)S(1)} collective-permute-done((bf16[256,1024]{1,0:T(8,128)(2,1)S(1)}, bf16[256,1024]{1,0:T(8,128)(2,1)S(1)}, u32[]{:S(2)}, u32[]{:S(2)}) %collective-permute-start.2) | collective-permute-done | bytes 524320 | tf_op jit(solution)/shard_map/ppermute | solution.py:456
  54.9 0.0 collective-permute-done.3.g_ref
  54.9 1.9 %far_rows.1 = (f32[8,256]{1,0:T(8,128)S(1)}, bf16[96,1024]{1,0:T(8,128)(2,1)S(1)}, bf16[96,1024]{1,0:T(8,128)(2,1)S(1)}, bf16[96,1024]{1,0:T(8,128)(2,1)}, bf16[...) custom-call(s32[1]{0:T(128)} %bitcast.me_ref, ...), custom_call_target="tpu_custom_call" | custom-call | flops 1048576 | bytes 1048576 | tf_op jit(solution)/shard_map/far_rows/pallas_call | solution.py:146
  56.8 1.5 %collective-permute-start.5 = (bf16[96,1024]{1,0:T(8,128)(2,1)S(1)}, bf16[96,1024]{1,0:T(8,128)(2,1)S(1)}, u32[]{:S(2)}, u32[]{:S(2)}) collective-permute-start(bf16[96,1024]{1,0:T(8,128)(2,1)S(1)} %get-tuple-element.67), channel_id=1, source_target_pairs={{0,2},{2,0},{4,6},{6,4},{8,10},{10,8},{12,14},{14,12},{1,3},{3,1},... | collective-permute-start | bytes 589832 | tf_op jit(solution)/shard_map/ppermute | solution.py:456
  58.3 2.0 %collective-permute-start.10 = (bf16[96,1024]{1,0:T(8,128)(2,1)}, bf16[96,1024]{1,0:T(8,128)(2,1)}, u32[]{:S(2)}, u32[]{:S(2)}) collective-permute-start(bf16[96,1024]{1,0:T(8,128)(2,1)} %get-tuple-element.74), channel_id=1, source_target_pairs={{0,6},{2,4},{4,2},{6,0},{8,14},{10,12},{12,10},{14,8},{1,7},{3,5},... | collective-permute-start | bytes 589832 | tf_op jit(solution)/shard_map/ppermute | solution.py:456
  60.3 4.9 %collective-permute-done.5.refs_5_ = bf16[96,1024]{1,0:T(8,128)(2,1)S(1)} collective-permute-done((bf16[96,1024]{1,0:T(8,128)(2,1)S(1)}, bf16[96,1024]{1,0:T(8,128)(2,1)S(1)}, u32[]{:S(2)}, u32[]{:S(2)}) %collective-permute-start.5) | collective-permute-done | bytes 196640 | tf_op jit(solution)/shard_map/ppermute | solution.py:456
  65.3 0.7 copy-done
  65.9 1.5 %collective-permute-start.6 = (bf16[160,1024]{1,0:T(8,128)(2,1)}, bf16[160,1024]{1,0:T(8,128)(2,1)S(1)}, u32[]{:S(2)}, u32[]{:S(2)}) collective-permute-start(bf16[160,1024]{1,0:T(8,128)(2,1)} %get-tuple-element.69), channel_id=1, source_target_pairs={{0,2},{2,0},{4,6},{6,4},{8,10},{10,8},{12,14},{14,12},{1,3},{3,1},... | collective-permute-start | bytes 983048 | tf_op jit(solution)/shard_map/ppermute | solution.py:456
  67.4 2.0 %collective-permute-start.8 = (bf16[160,1024]{1,0:T(8,128)(2,1)}, bf16[160,1024]{1,0:T(8,128)(2,1)}, u32[]{:S(2)}, u32[]{:S(2)}) collective-permute-start(bf16[160,1024]{1,0:T(8,128)(2,1)} %get-tuple-element.71), channel_id=1, source_target_pairs={{0,6},{2,4},{4,2},{6,0},{8,14},{10,12},{12,10},{14,8},{1,7},{3,5},... | collective-permute-start | bytes 983048 | tf_op jit(solution)/shard_map/ppermute | solution.py:456
  69.4 0.7 copy-done.2
  70.1 0.6 collective-permute-done.10.refs_7_
  70.7 0.9 copy-done.1
  71.6 0.9 copy-done.3
  72.5 8.4 %first_experts.1 = (bf16[96,1024]{1,0:T(8,128)(2,1)S(1)}, bf16[96,1024]{1,0:T(8,128)(2,1)S(1)}, bf16[96,1024]{1,0:T(8,128)(2,1)S(1)}, bf16[96,1024]{1,0:T(8,128)...) custom-call(s32[1]{0:T(128)} %bitcast.3.core_ref, ...), custom_call_target="tpu_custom_call" | custom-call | flops 1048576 | bytes 1048576 | tf_op jit(solution)/shard_map/first_experts/pallas_call | solution.py:294
  80.9 1.5 %collective-permute-start.11 = (bf16[96,1024]{1,0:T(8,128)(2,1)S(1)}, bf16[96,1024]{1,0:T(8,128)(2,1)S(1)}, u32[]{:S(2)}, u32[]{:S(2)}) collective-permute-start(bf16[96,1024]{1,0:T(8,128)(2,1)S(1)} %get-tuple-element.82), channel_id=1, source_target_pairs={{0,2},{2,0},{4,6},{6,4},{8,10},{10,8},{12,14},{14,12},{1,3},{3,1},... | collective-permute-start | bytes 589832 | tf_op jit(solution)/shard_map/ppermute | solution.py:456
  82.4 2.0 %collective-permute-start.13 = (bf16[96,1024]{1,0:T(8,128)(2,1)S(1)}, bf16[96,1024]{1,0:T(8,128)(2,1)S(1)}, u32[]{:S(2)}, u32[]{:S(2)}) collective-permute-start(bf16[96,1024]{1,0:T(8,128)(2,1)S(1)} %get-tuple-element.84), channel_id=1, source_target_pairs={{0,6},{2,4},{4,2},{6,0},{8,14},{10,12},{12,10},{14,8},{1,7},{3,5},... | collective-permute-start | bytes 589832 | tf_op jit(solution)/shard_map/ppermute | solution.py:456
  84.5 0.3 collective-permute-done.8.refs_7_
  84.7 11.8 %last_experts.1 = (bf16[96,1024]{1,0:T(8,128)(2,1)S(1)}, bf16[96,1024]{1,0:T(8,128)(2,1)S(1)}, bf16[96,1024]{1,0:T(8,128)(2,1)S(1)}, bf16[96,1024]{1,0:T(8,128)(...) custom-call(s32[1]{0:T(128)} %bitcast.3.core_ref, ...), custom_call_target="tpu_custom_call", output_to_operand_aliasing={{8}: (12, {}), {9}: (13, {})} | custom-call | flops 1048576 | bytes 1048576 | tf_op jit(solution)/shard_map/last_experts/pallas_call | solution.py:294
  96.6 1.5 %collective-permute-start.14 = (bf16[96,1024]{1,0:T(8,128)(2,1)S(1)}, bf16[96,1024]{1,0:T(8,128)(2,1)S(1)}, u32[]{:S(2)}, u32[]{:S(2)}) collective-permute-start(bf16[96,1024]{1,0:T(8,128)(2,1)S(1)} %get-tuple-element.86), channel_id=1, source_target_pairs={{0,2},{2,0},{4,6},{6,4},{8,10},{10,8},{12,14},{14,12},{1,3},{3,1},... | collective-permute-start | bytes 589832 | tf_op jit(solution)/shard_map/ppermute | solution.py:456
  98.1 0.0 collective-permute-start.15
  98.1 2.0 %collective-permute-start.16 = (bf16[96,1024]{1,0:T(8,128)(2,1)S(1)}, bf16[96,1024]{1,0:T(8,128)(2,1)S(1)}, u32[]{:S(2)}, u32[]{:S(2)}) collective-permute-start(bf16[96,1024]{1,0:T(8,128)(2,1)S(1)} %get-tuple-element.88), channel_id=1, source_target_pairs={{0,6},{2,4},{4,2},{6,0},{8,14},{10,12},{12,10},{14,8},{1,7},{3,5},... | collective-permute-start | bytes 589832 | tf_op jit(solution)/shard_map/ppermute | solution.py:456
  100.1 2.2 %collective-permute-done.14.refs_5_ = bf16[96,1024]{1,0:T(8,128)(2,1)S(1)} collective-permute-done((bf16[96,1024]{1,0:T(8,128)(2,1)S(1)}, bf16[96,1024]{1,0:T(8,128)(2,1)S(1)}, u32[]{:S(2)}, u32[]{:S(2)}) %collective-permute-start.14) | collective-permute-done | bytes 196640 | tf_op jit(solution)/shard_map/ppermute | solution.py:456
  102.3 1.5 %collective-permute-done.15.refs_6_ = bf16[96,1024]{1,0:T(8,128)(2,1)S(1)} collective-permute-done((bf16[96,1024]{1,0:T(8,128)(2,1)S(1)}, bf16[96,1024]{1,0:T(8,128)(2,1)S(1)}, u32[]{:S(2)}, u32[]{:S(2)}) %collective-permute-start.15) | collective-permute-done | bytes 196640 | tf_op jit(solution)/shard_map/ppermute | solution.py:456
  103.8 2.1 %collective-permute-done.16.refs_7_ = bf16[96,1024]{1,0:T(8,128)(2,1)S(1)} collective-permute-done((bf16[96,1024]{1,0:T(8,128)(2,1)S(1)}, bf16[96,1024]{1,0:T(8,128)(2,1)S(1)}, u32[]{:S(2)}, u32[]{:S(2)}) %collective-permute-start.16) | collective-permute-done | bytes 196640 | tf_op jit(solution)/shard_map/ppermute | solution.py:456
  105.9 0.7 relay_sum.1
  106.6 0.1 collective-permute-start.17
  106.7 1.6 %collective-permute-start.21 = (bf16[272,1024]{1,0:T(8,128)(2,1)S(1)}, bf16[272,1024]{1,0:T(8,128)(2,1)S(1)}, u32[]{:S(2)}, u32[]{:S(2)}) collective-permute-start(bf16[272,1024]{1,0:T(8,128)(2,1)S(1)} %relay_sum.1), channel_id=1, source_target_pairs={{0,8},{2,10},{4,12},{6,14},{8,0},{10,2},{12,4},{14,6},{1,9},{3,11}... | collective-permute-start | bytes 1671176 | tf_op jit(solution)/shard_map/ppermute | solution.py:456
  108.3 0.6 collective-permute-start.18
  108.9 2.0 %collective-permute-start.19 = (bf16[96,1024]{1,0:T(8,128)(2,1)S(1)}, bf16[96,1024]{1,0:T(8,128)(2,1)S(1)}, u32[]{:S(2)}, u32[]{:S(2)}) collective-permute-start(bf16[96,1024]{1,0:T(8,128)(2,1)S(1)} %get-tuple-element.98), channel_id=1, source_target_pairs={{0,4},{2,6},{4,0},{6,2},{8,12},{10,14},{12,8},{14,10},{1,5},{3,7},... | collective-permute-start | bytes 589832 | tf_op jit(solution)/shard_map/ppermute | solution.py:456
  110.9 0.8 collective-permute-start.20
  111.8 5.1 %collective-permute-done.17.other_ref = bf16[8,128,3072]{2,1,0:T(8,128)(2,1)S(1)} collective-permute-done((bf16[8,128,3072]{2,1,0:T(8,128)(2,1)S(1)}, bf16[8,128,3072]{2,1,0:T(8,128)(2,1)S(1)}, u32[]{:S(2)}, u32[]{:S(2)}) %collective-permute-start.17) | collective-permute-done | bytes 6291488 | tf_op jit(solution)/shard_map/ppermute | solution.py:459
  116.8 8.0 %weight_pass.1 = (bf16[8,512,1024]{2,1,0:T(8,128)(2,1)}, bf16[8,512,1024]{2,1,0:T(8,128)(2,1)}) custom-call(bf16[8,128,1024]{2,1,0:T(8,128)(2,1)S(1)} %get-tuple-element.78.mine_ref, bf16[8,128,3072]{2,1,0:T(8,128)(2,1)S(1)} %get-tuple-element.89.pack_ref, bf16[8,128,3072]{2,1,0:T(8,128)(2,1)S(1)} %collective-permute-done.17.other_ref), custom_call_target="tpu_custom_call" | custom-call | flops 1048576 | bytes 1048576 | tf_op jit(solution)/shard_map/weight_pass/pallas_call | solution.py:329
  124.9 0.6 collective-permute-done.19.refs_6_
  125.5 3.8 %collective-permute-done.20.refs_7_ = bf16[96,1024]{1,0:T(8,128)(2,1)S(1)} collective-permute-done((bf16[96,1024]{1,0:T(8,128)(2,1)S(1)}, bf16[96,1024]{1,0:T(8,128)(2,1)S(1)}, u32[]{:S(2)}, u32[]{:S(2)}) %collective-permute-start.20) | collective-permute-done | bytes 196640 | tf_op jit(solution)/shard_map/ppermute | solution.py:456
  129.2 0.9 near_sum.1
  130.1 4.5 %collective-permute-done.21.back_ref = bf16[272,1024]{1,0:T(8,128)(2,1)S(1)} collective-permute-done((bf16[272,1024]{1,0:T(8,128)(2,1)S(1)}, bf16[272,1024]{1,0:T(8,128)(2,1)S(1)}, u32[]{:S(2)}, u32[]{:S(2)}) %collective-permute-start.21) | collective-permute-done | bytes 557088 | tf_op jit(solution)/shard_map/ppermute | solution.py:456
  134.6 1.3 last_sum.1
  (15 shorter events, 0.0 us)
Async XLA Ops:
  1.9 53.0 %collective-permute-start.3 = (bf16[272,1024]{1,0:T(8,128)(2,1)S(1)}, bf16[272,1024]{1,0:T(8,128)(2,1)S(1)}, u32[]{:S(2)}, u32[]{:S(2)}) collective-permute-start(bf16[272,1024]{1,0:T(8,128)(2,1)S(1)} %get-tuple-element.55.g_ref), channel_id=1, source_target_pairs={{0,8},{2,10},{4,12},{6,14},{8,0},{10,2},{12,4},{14,6},{1,9},{3,11}... | collective-permute-start | bytes 1671176 | tf_op jit(solution)/shard_map/ppermute | solution.py:456
  7.0 34.5 %collective-permute-start = (bf16[256,1024]{1,0:T(8,128)(2,1)S(1)}, bf16[256,1024]{1,0:T(8,128)(2,1)S(1)}, u32[]{:S(2)}, u32[]{:S(2)}) collective-permute-start(bf16[256,1024]{1,0:T(8,128)(2,1)S(1)} %get-tuple-element.59), channel_id=1, source_target_pairs={{0,2},{2,0},{4,6},{6,4},{8,10},{10,8},{12,14},{14,12},{1,3},{3,1},... | collective-permute-start | bytes 1572872 | tf_op jit(solution)/shard_map/ppermute | solution.py:456
  8.6 36.9 %collective-permute-start.1 = (bf16[256,1024]{1,0:T(8,128)(2,1)S(1)}, bf16[256,1024]{1,0:T(8,128)(2,1)S(1)}, u32[]{:S(2)}, u32[]{:S(2)}) collective-permute-start(bf16[256,1024]{1,0:T(8,128)(2,1)S(1)} %get-tuple-element.60), channel_id=1, source_target_pairs={{0,4},{2,6},{4,0},{6,2},{8,12},{10,14},{12,8},{14,10},{1,5},{3,7},... | collective-permute-start | bytes 1572872 | tf_op jit(solution)/shard_map/ppermute | solution.py:456
  10.2 44.8 %collective-permute-start.2 = (bf16[256,1024]{1,0:T(8,128)(2,1)S(1)}, bf16[256,1024]{1,0:T(8,128)(2,1)S(1)}, u32[]{:S(2)}, u32[]{:S(2)}) collective-permute-start(bf16[256,1024]{1,0:T(8,128)(2,1)S(1)} %get-tuple-element.61), channel_id=1, source_target_pairs={{0,6},{2,4},{4,2},{6,0},{8,14},{10,12},{12,10},{14,8},{1,7},{3,5},... | collective-permute-start | bytes 1572872 | tf_op jit(solution)/shard_map/ppermute | solution.py:456
  10.6 44.4 %collective-permute-start.4 = (bf16[256,1024]{1,0:T(8,128)(2,1)}, bf16[256,1024]{1,0:T(8,128)(2,1)S(1)}, u32[]{:S(2)}, u32[]{:S(2)}) collective-permute-start(bf16[256,1024]{1,0:T(8,128)(2,1)} %x_hbm.1), channel_id=1, source_target_pairs={{0,8},{2,10},{4,12},{6,14},{8,0},{10,2},{12,4},{14,6},{1,9},{3,11}... | collective-permute-start | bytes 1572872 | tf_op jit(solution)/shard_map/ppermute | solution.py:456
  56.8 8.4 %collective-permute-start.5 = (bf16[96,1024]{1,0:T(8,128)(2,1)S(1)}, bf16[96,1024]{1,0:T(8,128)(2,1)S(1)}, u32[]{:S(2)}, u32[]{:S(2)}) collective-permute-start(bf16[96,1024]{1,0:T(8,128)(2,1)S(1)} %get-tuple-element.67), channel_id=1, source_target_pairs={{0,2},{2,0},{4,6},{6,4},{8,10},{10,8},{12,14},{14,12},{1,3},{3,1},... | collective-permute-start | bytes 589832 | tf_op jit(solution)/shard_map/ppermute | solution.py:456
  58.3 11.1 %collective-permute-start.9 = (bf16[96,1024]{1,0:T(8,128)(2,1)}, bf16[96,1024]{1,0:T(8,128)(2,1)S(1)}, u32[]{:S(2)}, u32[]{:S(2)}) collective-permute-start(bf16[96,1024]{1,0:T(8,128)(2,1)} %get-tuple-element.73), channel_id=1, source_target_pairs={{0,4},{2,6},{4,0},{6,2},{8,12},{10,14},{12,8},{14,10},{1,5},{3,7},... | collective-permute-start | bytes 589832 | tf_op jit(solution)/shard_map/ppermute | solution.py:456
  58.3 12.4 %collective-permute-start.10 = (bf16[96,1024]{1,0:T(8,128)(2,1)}, bf16[96,1024]{1,0:T(8,128)(2,1)}, u32[]{:S(2)}, u32[]{:S(2)}) collective-permute-start(bf16[96,1024]{1,0:T(8,128)(2,1)} %get-tuple-element.74), channel_id=1, source_target_pairs={{0,6},{2,4},{4,2},{6,0},{8,14},{10,12},{12,10},{14,8},{1,7},{3,5},... | collective-permute-start | bytes 589832 | tf_op jit(solution)/shard_map/ppermute | solution.py:456
  65.3 0.7 copy-start
  65.9 16.5 %collective-permute-start.6 = (bf16[160,1024]{1,0:T(8,128)(2,1)}, bf16[160,1024]{1,0:T(8,128)(2,1)S(1)}, u32[]{:S(2)}, u32[]{:S(2)}) collective-permute-start(bf16[160,1024]{1,0:T(8,128)(2,1)} %get-tuple-element.69), channel_id=1, source_target_pairs={{0,2},{2,0},{4,6},{6,4},{8,10},{10,8},{12,14},{14,12},{1,3},{3,1},... | collective-permute-start | bytes 983048 | tf_op jit(solution)/shard_map/ppermute | solution.py:456
  67.4 17.1 %collective-permute-start.7 = (bf16[160,1024]{1,0:T(8,128)(2,1)}, bf16[160,1024]{1,0:T(8,128)(2,1)S(1)}, u32[]{:S(2)}, u32[]{:S(2)}) collective-permute-start(bf16[160,1024]{1,0:T(8,128)(2,1)} %get-tuple-element.70), channel_id=1, source_target_pairs={{0,4},{2,6},{4,0},{6,2},{8,12},{10,14},{12,8},{14,10},{1,5},{3,7},... | collective-permute-start | bytes 983048 | tf_op jit(solution)/shard_map/ppermute | solution.py:456
  67.4 17.3 %collective-permute-start.8 = (bf16[160,1024]{1,0:T(8,128)(2,1)}, bf16[160,1024]{1,0:T(8,128)(2,1)}, u32[]{:S(2)}, u32[]{:S(2)}) collective-permute-start(bf16[160,1024]{1,0:T(8,128)(2,1)} %get-tuple-element.71), channel_id=1, source_target_pairs={{0,6},{2,4},{4,2},{6,0},{8,14},{10,12},{12,10},{14,8},{1,7},{3,5},... | collective-permute-start | bytes 983048 | tf_op jit(solution)/shard_map/ppermute | solution.py:456
  69.4 0.7 copy-start.2
  70.7 0.9 copy-start.1
  71.6 0.9 copy-start.3
  80.9 17.2 %collective-permute-start.11 = (bf16[96,1024]{1,0:T(8,128)(2,1)S(1)}, bf16[96,1024]{1,0:T(8,128)(2,1)S(1)}, u32[]{:S(2)}, u32[]{:S(2)}) collective-permute-start(bf16[96,1024]{1,0:T(8,128)(2,1)S(1)} %get-tuple-element.82), channel_id=1, source_target_pairs={{0,2},{2,0},{4,6},{6,4},{8,10},{10,8},{12,14},{14,12},{1,3},{3,1},... | collective-permute-start | bytes 589832 | tf_op jit(solution)/shard_map/ppermute | solution.py:456
  82.4 17.7 %collective-permute-start.12 = (bf16[96,1024]{1,0:T(8,128)(2,1)S(1)}, bf16[96,1024]{1,0:T(8,128)(2,1)S(1)}, u32[]{:S(2)}, u32[]{:S(2)}) collective-permute-start(bf16[96,1024]{1,0:T(8,128)(2,1)S(1)} %get-tuple-element.83), channel_id=1, source_target_pairs={{0,4},{2,6},{4,0},{6,2},{8,12},{10,14},{12,8},{14,10},{1,5},{3,7},... | collective-permute-start | bytes 589832 | tf_op jit(solution)/shard_map/ppermute | solution.py:456
  82.4 17.7 %collective-permute-start.13 = (bf16[96,1024]{1,0:T(8,128)(2,1)S(1)}, bf16[96,1024]{1,0:T(8,128)(2,1)S(1)}, u32[]{:S(2)}, u32[]{:S(2)}) collective-permute-start(bf16[96,1024]{1,0:T(8,128)(2,1)S(1)} %get-tuple-element.84), channel_id=1, source_target_pairs={{0,6},{2,4},{4,2},{6,0},{8,14},{10,12},{12,10},{14,8},{1,7},{3,5},... | collective-permute-start | bytes 589832 | tf_op jit(solution)/shard_map/ppermute | solution.py:456
  96.6 5.7 %collective-permute-start.14 = (bf16[96,1024]{1,0:T(8,128)(2,1)S(1)}, bf16[96,1024]{1,0:T(8,128)(2,1)S(1)}, u32[]{:S(2)}, u32[]{:S(2)}) collective-permute-start(bf16[96,1024]{1,0:T(8,128)(2,1)S(1)} %get-tuple-element.86), channel_id=1, source_target_pairs={{0,2},{2,0},{4,6},{6,4},{8,10},{10,8},{12,14},{14,12},{1,3},{3,1},... | collective-permute-start | bytes 589832 | tf_op jit(solution)/shard_map/ppermute | solution.py:456
  98.1 5.7 %collective-permute-start.15 = (bf16[96,1024]{1,0:T(8,128)(2,1)S(1)}, bf16[96,1024]{1,0:T(8,128)(2,1)S(1)}, u32[]{:S(2)}, u32[]{:S(2)}) collective-permute-start(bf16[96,1024]{1,0:T(8,128)(2,1)S(1)} %get-tuple-element.87), channel_id=1, source_target_pairs={{0,4},{2,6},{4,0},{6,2},{8,12},{10,14},{12,8},{14,10},{1,5},{3,7},... | collective-permute-start | bytes 589832 | tf_op jit(solution)/shard_map/ppermute | solution.py:456
  98.1 7.7 %collective-permute-start.16 = (bf16[96,1024]{1,0:T(8,128)(2,1)S(1)}, bf16[96,1024]{1,0:T(8,128)(2,1)S(1)}, u32[]{:S(2)}, u32[]{:S(2)}) collective-permute-start(bf16[96,1024]{1,0:T(8,128)(2,1)S(1)} %get-tuple-element.88), channel_id=1, source_target_pairs={{0,6},{2,4},{4,2},{6,0},{8,14},{10,12},{12,10},{14,8},{1,7},{3,5},... | collective-permute-start | bytes 589832 | tf_op jit(solution)/shard_map/ppermute | solution.py:456
  106.6 10.2 %collective-permute-start.17 = (bf16[8,128,3072]{2,1,0:T(8,128)(2,1)S(1)}, bf16[8,128,3072]{2,1,0:T(8,128)(2,1)S(1)}, u32[]{:S(2)}, u32[]{:S(2)}) collective-permute-start(bf16[8,128,3072]{2,1,0:T(8,128)(2,1)S(1)} %get-tuple-element.89.pack_ref), channel_id=1, source_target_pairs={{0,1},{1,0},{2,3},{3,2},{4,5},{5,4},{6,7},{7,6},{8,9},{9,8},{10,11... | collective-permute-start | bytes 18874376 | tf_op jit(solution)/shard_map/ppermute | solution.py:459
  106.7 27.9 %collective-permute-start.21 = (bf16[272,1024]{1,0:T(8,128)(2,1)S(1)}, bf16[272,1024]{1,0:T(8,128)(2,1)S(1)}, u32[]{:S(2)}, u32[]{:S(2)}) collective-permute-start(bf16[272,1024]{1,0:T(8,128)(2,1)S(1)} %relay_sum.1), channel_id=1, source_target_pairs={{0,8},{2,10},{4,12},{6,14},{8,0},{10,2},{12,4},{14,6},{1,9},{3,11}... | collective-permute-start | bytes 1671176 | tf_op jit(solution)/shard_map/ppermute | solution.py:456
  108.3 16.6 %collective-permute-start.18 = (bf16[96,1024]{1,0:T(8,128)(2,1)S(1)}, bf16[96,1024]{1,0:T(8,128)(2,1)S(1)}, u32[]{:S(2)}, u32[]{:S(2)}) collective-permute-start(bf16[96,1024]{1,0:T(8,128)(2,1)S(1)} %get-tuple-element.97), channel_id=1, source_target_pairs={{0,2},{2,0},{4,6},{6,4},{8,10},{10,8},{12,14},{14,12},{1,3},{3,1},... | collective-permute-start | bytes 589832 | tf_op jit(solution)/shard_map/ppermute | solution.py:456
  108.9 16.6 %collective-permute-start.19 = (bf16[96,1024]{1,0:T(8,128)(2,1)S(1)}, bf16[96,1024]{1,0:T(8,128)(2,1)S(1)}, u32[]{:S(2)}, u32[]{:S(2)}) collective-permute-start(bf16[96,1024]{1,0:T(8,128)(2,1)S(1)} %get-tuple-element.98), channel_id=1, source_target_pairs={{0,4},{2,6},{4,0},{6,2},{8,12},{10,14},{12,8},{14,10},{1,5},{3,7},... | collective-permute-start | bytes 589832 | tf_op jit(solution)/shard_map/ppermute | solution.py:456
  110.9 18.3 %collective-permute-start.20 = (bf16[96,1024]{1,0:T(8,128)(2,1)S(1)}, bf16[96,1024]{1,0:T(8,128)(2,1)S(1)}, u32[]{:S(2)}, u32[]{:S(2)}) collective-permute-start(bf16[96,1024]{1,0:T(8,128)(2,1)S(1)} %get-tuple-element.99), channel_id=1, source_target_pairs={{0,6},{2,4},{4,2},{6,0},{8,14},{10,12},{12,10},{14,8},{1,7},{3,5},... | collective-permute-start | bytes 589832 | tf_op jit(solution)/shard_map/ppermute | solution.py:456

commit v3 on v2

--- a/solution.py
+++ b/solution.py
@@ -121,17 +121,13 @@
     return pl.BlockSpec(shape, lambda j: (j,) + (0,) * (len(shape) - 1))
 
 
-def rows_kernel(peers, sizes, me_ref, g_ref, x_ref, facts_ref, *rows_refs):
-    tokens, slots = x_ref.shape[0], sum(sizes)
+def rows_kernel(peers, slots, start, me_ref, g_ref, x_ref, facts_ref, *rows_refs):
+    tokens, size = x_ref.shape[0], rows_refs[0].shape[0] // 2
     tgt, gates = facts_of(g_ref, tokens)
     for m in range(peers):
-        select, gate = select_slots(tgt, gates, (me_ref[0] ^ m) * slots, slots)
-        x = dot(select, x_ref[...], NN).astype(BF)
-        d = (gate * dot(select, g_ref[0:tokens], NN)).astype(BF)
-        for i, size in enumerate(sizes):
-            at = slice(sum(sizes[:i]), sum(sizes[:i]) + size)
-            rows_refs[i * peers + m][0:size] = x[at]
-            rows_refs[i * peers + m][size:] = d[at]
+        select, gate = select_slots(tgt, gates, (me_ref[0] ^ m) * slots + start, size)
+        rows_refs[m][0:size] = dot(select, x_ref[...], NN).astype(BF)
+        rows_refs[m][size:] = (gate * dot(select, g_ref[0:tokens], NN)).astype(BF)
     facts_ref[0:2] = jnp.concatenate(tgt, axis=0).astype(F32)
     facts_ref[2:4] = jnp.concatenate(gates, axis=0)
     facts_ref[4:8] = jnp.zeros((4, tokens), F32)
@@ -141,19 +137,18 @@
 VECTORS = pl.BlockSpec(memory_space=pltpu.VMEM)
 
 
-def rows_pass(name, sizes, me, g, x, peers):
+def rows_pass(name, slots, start, size, me, g, x, peers):
     tokens, width = x.shape
     out = pl.pallas_call(
-        functools.partial(rows_kernel, peers, sizes),
-        out_shape=[jax.ShapeDtypeStruct((8, tokens), F32)]
-        + [jax.ShapeDtypeStruct((2 * size, width), BF) for size in sizes for _ in range(peers)],
+        functools.partial(rows_kernel, peers, slots, start),
+        out_shape=[jax.ShapeDtypeStruct((8, tokens), F32)] + [jax.ShapeDtypeStruct((2 * size, width), BF)] * peers,
         in_specs=[SCALARS] + [VECTORS] * 2,
-        out_specs=[VECTORS] * (1 + len(sizes) * peers),
+        out_specs=[VECTORS] * (1 + peers),
         compiler_params=params(),
         cost_estimate=COST,
         name=name,
     )(me, g, x)
-    return out[0], *(list(out[1 + i * peers : 1 + (i + 1) * peers]) for i in range(len(sizes)))
+    return out[0], list(out[1:])
 
 
 def fetch(weight_hbm, weight_ref, sem, first=0):
@@ -464,14 +459,13 @@
     g_near, x_near = prepare(routes.T, gate_values.T, grad_out, tokens)
     g_far = swap(g_near, half)
     x_far = swap(tokens, half)
-    facts, near = rows_pass("near_rows", (slots,), me, g_near, x_near, half)
+    facts, near = rows_pass("near_rows", slots, 0, slots, me, g_near, x_near, half)
     near = deal(near)
     weights = turned(up_weight), turned(down_weight)
-    facts_far, far_first, far_last = rows_pass(
-        "far_rows", (first, slots - first), me, after(g_far, near, weights), x_far, half
-    )
+    facts_far, far_first = rows_pass("far_first", slots, 0, first, me, after(g_far, near, weights), x_far, half)
     far_first = deal(far_first)
-    far_last = deal(after(far_last, far_first[1]))
+    _, far_last = rows_pass("far_last", slots, first, slots - first, me, after(g_far, far_first[1]), x_far, half)
+    far_last = deal(far_last)
 
     gx_first, part, pack, mine = block_pass(0, core, *weights, near, far_first)
     gx_first = deal(gx_first)

time: 136 us -> 137 us (level)
  Pallas kernels: 66.3 us -> 68 us
  local copies, waits for them, and re-layouts: 3.2 us -> 1.59 us
    pallas_call x2 -> x3, Pallas kernels: 2.9 us -> 4.61 us  [rows_pass(): pl.pallas_call(functools.partial(rows_kernel, peers, slots, start), out_s...]
    unnamed x8 -> x4, local copies, waits for them, and re-layouts: 3.2 us -> 1.59 us
  transfers between devices with their start and end apart: 22 -> 22, of which waited for: 12 -> 11; matrix products, arithmetic and copies ran while one was open for 0% -> 0% of each run, Pallas kernels for 45% -> 46%
where the time goes in v3:
time: 137 us; the launch traced here: 136 us
  Pallas kernels  68 us (50%)
  waiting for transfers between devices  38.7 us (28%)
  starting transfers between devices  27.2 us (20%)
  local copies, waits for them, and re-layouts  1.59 us (1%)
    ppermute x21, waiting for transfers between devices, swap(): return lax.ppermute(value, 'expert', [(i, i ^ m) for i in range(chips)])  33.9 us
    pallas_call x2, Pallas kernels, turned(): pl.pallas_call(turn_kernel, grid=(experts,), out_shape=pltpu.HBM((experts...  30.9 us
    ppermute x21, starting transfers between devices, swap(): return lax.ppermute(value, 'expert', [(i, i ^ m) for i in range(chips)])  27.2 us
    pallas_call x2, Pallas kernels, block_pass(): pl.pallas_call(functools.partial(block_kernel, peers, which), out_shape=[...  20.3 us
    pallas_call x1, Pallas kernels, weight_pass(): pl.pallas_call(weight_kernel, grid=(experts,), out_shape=[jax.ShapeDtypeS...  8.05 us
    ppermute x1, waiting for transfers between devices, swap_core(): return lax.ppermute(value, 'dp', [(0, 1), (1, 0)])  4.75 us
    pallas_call x3, Pallas kernels, rows_pass(): pl.pallas_call(functools.partial(rows_kernel, peers, slots, start), out_s...  4.61 us
  transfers between devices with their start and end apart: 22, of which 11 were waited for; matrix products, arithmetic and copies ran while one was open for 0% of the time, Pallas kernels for 46%

profile of v3, /device:TPU:0, one launch (start us, length us, event | category | flops | bytes accessed | tf_op | source)
XLA Modules:
  0.0 136.2 jit_solution(6331170444112429425)
XLA Ops:
  0.6 1.3 prepare.1
  1.9 4.1 %collective-permute-start.3 = (bf16[272,1024]{1,0:T(8,128)(2,1)S(1)}, bf16[272,1024]{1,0:T(8,128)(2,1)S(1)}, u32[]{:S(2)}, u32[]{:S(2)}) collective-permute-start(bf16[272,1024]{1,0:T(8,128)(2,1)S(1)} %get-tuple-element.52.g_ref), channel_id=1, source_target_pairs={{0,8},{2,10},{4,12},{6,14},{8,0},{10,2},{12,4},{14,6},{1,9},{3,11}... | collective-permute-start | bytes 1671176 | tf_op jit(solution)/shard_map/ppermute | solution.py:451
  6.0 1.0 near_rows.1
  7.0 1.6 %collective-permute-start = (bf16[256,1024]{1,0:T(8,128)(2,1)S(1)}, bf16[256,1024]{1,0:T(8,128)(2,1)S(1)}, u32[]{:S(2)}, u32[]{:S(2)}) collective-permute-start(bf16[256,1024]{1,0:T(8,128)(2,1)S(1)} %get-tuple-element.56), channel_id=1, source_target_pairs={{0,2},{2,0},{4,6},{6,4},{8,10},{10,8},{12,14},{14,12},{1,3},{3,1},... | collective-permute-start | bytes 1572872 | tf_op jit(solution)/shard_map/ppermute | solution.py:451
  8.6 1.6 %collective-permute-start.1 = (bf16[256,1024]{1,0:T(8,128)(2,1)S(1)}, bf16[256,1024]{1,0:T(8,128)(2,1)S(1)}, u32[]{:S(2)}, u32[]{:S(2)}) collective-permute-start(bf16[256,1024]{1,0:T(8,128)(2,1)S(1)} %get-tuple-element.57), channel_id=1, source_target_pairs={{0,4},{2,6},{4,0},{6,2},{8,12},{10,14},{12,8},{14,10},{1,5},{3,7},... | collective-permute-start | bytes 1572872 | tf_op jit(solution)/shard_map/ppermute | solution.py:451
  10.2 0.4 collective-permute-start.2
  10.6 0.0 collective-permute-start.4
  10.6 15.5 %turned.2.up_hbm = bf16[8,1024,1024]{2,1,0:T(8,128)(2,1)} custom-call(bf16[8,1024,1024]{2,1,0:T(8,128)(2,1)} %weight_ref.2), custom_call_target="tpu_custom_call" | custom-call | flops 1048576 | bytes 1048576 | tf_op jit(solution)/shard_map/turned/pallas_call | solution.py:170
  26.1 15.5 %turned.3.down_hbm = bf16[8,1024,1024]{2,1,0:T(8,128)(2,1)} custom-call(bf16[8,1024,1024]{2,1,0:T(8,128)(2,1)} %weight_ref.3), custom_call_target="tpu_custom_call" | custom-call | flops 1048576 | bytes 1048576 | tf_op jit(solution)/shard_map/turned/pallas_call | solution.py:170
  41.5 0.0 collective-permute-done.refs_1_
  41.5 3.9 %collective-permute-done.1.refs_2_ = bf16[256,1024]{1,0:T(8,128)(2,1)S(1)} collective-permute-done((bf16[256,1024]{1,0:T(8,128)(2,1)S(1)}, bf16[256,1024]{1,0:T(8,128)(2,1)S(1)}, u32[]{:S(2)}, u32[]{:S(2)}) %collective-permute-start.1) | collective-permute-done | bytes 524320 | tf_op jit(solution)/shard_map/ppermute | solution.py:451
  45.5 9.5 %collective-permute-done.2.refs_3_ = bf16[256,1024]{1,0:T(8,128)(2,1)S(1)} collective-permute-done((bf16[256,1024]{1,0:T(8,128)(2,1)S(1)}, bf16[256,1024]{1,0:T(8,128)(2,1)S(1)}, u32[]{:S(2)}, u32[]{:S(2)}) %collective-permute-start.2) | collective-permute-done | bytes 524320 | tf_op jit(solution)/shard_map/ppermute | solution.py:451
  54.9 0.0 collective-permute-done.4.x_ref
  54.9 1.7 %far_first.1 = (f32[8,256]{1,0:T(8,128)S(1)}, bf16[96,1024]{1,0:T(8,128)(2,1)S(1)}, bf16[96,1024]{1,0:T(8,128)(2,1)S(1)}, bf16[96,1024]{1,0:T(8,128)(2,1)}, bf16[96,1024]{1,0:T(8,128)(2,1)}) custom-call(s32[1]{0:T(128)} %bitcast.me_ref, bf16[272,1024]{1,0:T(8,128)(2,1)S(1)} %collective-permute-done.3.g_ref, bf16[256,1024]{1,0:T(8,128)(2,1)S(1)} %collective-permute-done.4.x_ref), custom_call_target="tpu_custom_call" | custom-call | flops 1048576 | bytes 1048576 | tf_op jit(solution)/shard_map/far_first/pallas_call | solution.py:142
  56.7 1.5 %collective-permute-start.5 = (bf16[96,1024]{1,0:T(8,128)(2,1)S(1)}, bf16[96,1024]{1,0:T(8,128)(2,1)S(1)}, u32[]{:S(2)}, u32[]{:S(2)}) collective-permute-start(bf16[96,1024]{1,0:T(8,128)(2,1)S(1)} %get-tuple-element.60), channel_id=1, source_target_pairs={{0,2},{2,0},{4,6},{6,4},{8,10},{10,8},{12,14},{14,12},{1,3},{3,1},... | collective-permute-start | bytes 589832 | tf_op jit(solution)/shard_map/ppermute | solution.py:451
  58.2 2.0 %collective-permute-start.10 = (bf16[96,1024]{1,0:T(8,128)(2,1)}, bf16[96,1024]{1,0:T(8,128)(2,1)}, u32[]{:S(2)}, u32[]{:S(2)}) collective-permute-start(bf16[96,1024]{1,0:T(8,128)(2,1)} %get-tuple-element.68), channel_id=1, source_target_pairs={{0,6},{2,4},{4,2},{6,0},{8,14},{10,12},{12,10},{14,8},{1,7},{3,5},... | collective-permute-start | bytes 589832 | tf_op jit(solution)/shard_map/ppermute | solution.py:451
  60.2 4.3 %collective-permute-done.5.refs_5_ = bf16[96,1024]{1,0:T(8,128)(2,1)S(1)} collective-permute-done((bf16[96,1024]{1,0:T(8,128)(2,1)S(1)}, bf16[96,1024]{1,0:T(8,128)(2,1)S(1)}, u32[]{:S(2)}, u32[]{:S(2)}) %collective-permute-start.5) | collective-permute-done | bytes 196640 | tf_op jit(solution)/shard_map/ppermute | solution.py:451
  64.4 0.7 copy-done
  65.1 1.9 %far_last.1 = (f32[8,256]{1,0:T(8,128)}, bf16[160,1024]{1,0:T(8,128)(2,1)S(1)}, bf16[160,1024]{1,0:T(8,128)(2,1)}, bf16[160,1024]{1,0:T(8,128)(2,1)}, bf16[160,1024]{1,0:T(8,128)(2,1)}) custom-call(s32[1]{0:T(128)} %bitcast.me_ref, bf16[272,1024]{1,0:T(8,128)(2,1)S(1)} %collective-permute-done.3.g_ref, bf16[256,1024]{1,0:T(8,128)(2,1)S(1)} %collective-permute-done.4.x_ref), custom_call_target="tpu_custom_call" | custom-call | flops 1048576 | bytes 1048576 | tf_op jit(solution)/shard_map/far_last/pallas_call | solution.py:142
  67.0 1.5 %collective-permute-start.6 = (bf16[160,1024]{1,0:T(8,128)(2,1)}, bf16[160,1024]{1,0:T(8,128)(2,1)S(1)}, u32[]{:S(2)}, u32[]{:S(2)}) collective-permute-start(bf16[160,1024]{1,0:T(8,128)(2,1)} %get-tuple-element.63), channel_id=1, source_target_pairs={{0,2},{2,0},{4,6},{6,4},{8,10},{10,8},{12,14},{14,12},{1,3},{3,1},... | collective-permute-start | bytes 983048 | tf_op jit(solution)/shard_map/ppermute | solution.py:451
  68.4 0.0 collective-permute-start.7
  68.4 2.0 %collective-permute-start.8 = (bf16[160,1024]{1,0:T(8,128)(2,1)}, bf16[160,1024]{1,0:T(8,128)(2,1)}, u32[]{:S(2)}, u32[]{:S(2)}) collective-permute-start(bf16[160,1024]{1,0:T(8,128)(2,1)} %get-tuple-element.65), channel_id=1, source_target_pairs={{0,6},{2,4},{4,2},{6,0},{8,14},{10,12},{12,10},{14,8},{1,7},{3,5},... | collective-permute-start | bytes 983048 | tf_op jit(solution)/shard_map/ppermute | solution.py:451
  70.5 0.0 collective-permute-done.10.refs_7_
  70.5 0.9 copy-done.1
  71.4 8.4 %first_experts.1 = (bf16[96,1024]{1,0:T(8,128)(2,1)S(1)}, bf16[96,1024]{1,0:T(8,128)(2,1)S(1)}, bf16[96,1024]{1,0:T(8,128)(2,1)S(1)}, bf16[96,1024]{1,0:T(8,128)...) custom-call(s32[1]{0:T(128)} %bitcast.3.core_ref, ...), custom_call_target="tpu_custom_call" | custom-call | flops 1048576 | bytes 1048576 | tf_op jit(solution)/shard_map/first_experts/pallas_call | solution.py:289
  79.8 1.5 %collective-permute-start.11 = (bf16[96,1024]{1,0:T(8,128)(2,1)S(1)}, bf16[96,1024]{1,0:T(8,128)(2,1)S(1)}, u32[]{:S(2)}, u32[]{:S(2)}) collective-permute-start(bf16[96,1024]{1,0:T(8,128)(2,1)S(1)} %get-tuple-element.76), channel_id=1, source_target_pairs={{0,2},{2,0},{4,6},{6,4},{8,10},{10,8},{12,14},{14,12},{1,3},{3,1},... | collective-permute-start | bytes 589832 | tf_op jit(solution)/shard_map/ppermute | solution.py:451
  81.4 2.0 %collective-permute-start.13 = (bf16[96,1024]{1,0:T(8,128)(2,1)S(1)}, bf16[96,1024]{1,0:T(8,128)(2,1)S(1)}, u32[]{:S(2)}, u32[]{:S(2)}) collective-permute-start(bf16[96,1024]{1,0:T(8,128)(2,1)S(1)} %get-tuple-element.78), channel_id=1, source_target_pairs={{0,6},{2,4},{4,2},{6,0},{8,14},{10,12},{12,10},{14,8},{1,7},{3,5},... | collective-permute-start | bytes 589832 | tf_op jit(solution)/shard_map/ppermute | solution.py:451
  83.4 1.7 %collective-permute-done.8.refs_7_ = bf16[160,1024]{1,0:T(8,128)(2,1)} collective-permute-done((bf16[160,1024]{1,0:T(8,128)(2,1)}, bf16[160,1024]{1,0:T(8,128)(2,1)}, u32[]{:S(2)}, u32[]{:S(2)}) %collective-permute-start.8) | collective-permute-done | bytes 327712 | tf_op jit(solution)/shard_map/ppermute | solution.py:451
  85.1 11.8 %last_experts.1 = (bf16[96,1024]{1,0:T(8,128)(2,1)S(1)}, bf16[96,1024]{1,0:T(8,128)(2,1)S(1)}, bf16[96,1024]{1,0:T(8,128)(2,1)S(1)}, bf16[96,1024]{1,0:T(8,128)(...) custom-call(s32[1]{0:T(128)} %bitcast.3.core_ref, ...), custom_call_target="tpu_custom_call", output_to_operand_aliasing={{8}: (12, {}), {9}: (13, {})} | custom-call | flops 1048576 | bytes 1048576 | tf_op jit(solution)/shard_map/last_experts/pallas_call | solution.py:289
  96.9 1.6 %collective-permute-start.14 = (bf16[96,1024]{1,0:T(8,128)(2,1)S(1)}, bf16[96,1024]{1,0:T(8,128)(2,1)S(1)}, u32[]{:S(2)}, u32[]{:S(2)}) collective-permute-start(bf16[96,1024]{1,0:T(8,128)(2,1)S(1)} %get-tuple-element.80), channel_id=1, source_target_pairs={{0,2},{2,0},{4,6},{6,4},{8,10},{10,8},{12,14},{14,12},{1,3},{3,1},... | collective-permute-start | bytes 589832 | tf_op jit(solution)/shard_map/ppermute | solution.py:451
  98.5 0.0 collective-permute-start.15
  98.5 2.0 %collective-permute-start.16 = (bf16[96,1024]{1,0:T(8,128)(2,1)S(1)}, bf16[96,1024]{1,0:T(8,128)(2,1)S(1)}, u32[]{:S(2)}, u32[]{:S(2)}) collective-permute-start(bf16[96,1024]{1,0:T(8,128)(2,1)S(1)} %get-tuple-element.82), channel_id=1, source_target_pairs={{0,6},{2,4},{4,2},{6,0},{8,14},{10,12},{12,10},{14,8},{1,7},{3,5},... | collective-permute-start | bytes 589832 | tf_op jit(solution)/shard_map/ppermute | solution.py:451
  100.5 2.2 %collective-permute-done.14.refs_5_ = bf16[96,1024]{1,0:T(8,128)(2,1)S(1)} collective-permute-done((bf16[96,1024]{1,0:T(8,128)(2,1)S(1)}, bf16[96,1024]{1,0:T(8,128)(2,1)S(1)}, u32[]{:S(2)}, u32[]{:S(2)}) %collective-permute-start.14) | collective-permute-done | bytes 196640 | tf_op jit(solution)/shard_map/ppermute | solution.py:451
  102.7 1.5 %collective-permute-done.15.refs_6_ = bf16[96,1024]{1,0:T(8,128)(2,1)S(1)} collective-permute-done((bf16[96,1024]{1,0:T(8,128)(2,1)S(1)}, bf16[96,1024]{1,0:T(8,128)(2,1)S(1)}, u32[]{:S(2)}, u32[]{:S(2)}) %collective-permute-start.15) | collective-permute-done | bytes 196640 | tf_op jit(solution)/shard_map/ppermute | solution.py:451
  104.1 2.1 %collective-permute-done.16.refs_7_ = bf16[96,1024]{1,0:T(8,128)(2,1)S(1)} collective-permute-done((bf16[96,1024]{1,0:T(8,128)(2,1)S(1)}, bf16[96,1024]{1,0:T(8,128)(2,1)S(1)}, u32[]{:S(2)}, u32[]{:S(2)}) %collective-permute-start.16) | collective-permute-done | bytes 196640 | tf_op jit(solution)/shard_map/ppermute | solution.py:451
  106.2 0.7 relay_sum.1
  107.0 0.1 collective-permute-start.17
  107.0 1.9 %collective-permute-start.21 = (bf16[272,1024]{1,0:T(8,128)(2,1)S(1)}, bf16[272,1024]{1,0:T(8,128)(2,1)S(1)}, u32[]{:S(2)}, u32[]{:S(2)}) collective-permute-start(bf16[272,1024]{1,0:T(8,128)(2,1)S(1)} %relay_sum.1), channel_id=1, source_target_pairs={{0,8},{2,10},{4,12},{6,14},{8,0},{10,2},{12,4},{14,6},{1,9},{3,11}... | collective-permute-start | bytes 1671176 | tf_op jit(solution)/shard_map/ppermute | solution.py:451
  108.9 0.7 collective-permute-start.18
  109.7 1.9 %collective-permute-start.19 = (bf16[96,1024]{1,0:T(8,128)(2,1)S(1)}, bf16[96,1024]{1,0:T(8,128)(2,1)S(1)}, u32[]{:S(2)}, u32[]{:S(2)}) collective-permute-start(bf16[96,1024]{1,0:T(8,128)(2,1)S(1)} %get-tuple-element.92), channel_id=1, source_target_pairs={{0,4},{2,6},{4,0},{6,2},{8,12},{10,14},{12,8},{14,10},{1,5},{3,7},... | collective-permute-start | bytes 589832 | tf_op jit(solution)/shard_map/ppermute | solution.py:451
  111.6 0.8 collective-permute-start.20
  112.4 4.7 %collective-permute-done.17.other_ref = bf16[8,128,3072]{2,1,0:T(8,128)(2,1)S(1)} collective-permute-done((bf16[8,128,3072]{2,1,0:T(8,128)(2,1)S(1)}, bf16[8,128,3072]{2,1,0:T(8,128)(2,1)S(1)}, u32[]{:S(2)}, u32[]{:S(2)}) %collective-permute-start.17) | collective-permute-done | bytes 6291488 | tf_op jit(solution)/shard_map/ppermute | solution.py:454
  117.2 8.0 %weight_pass.1 = (bf16[8,512,1024]{2,1,0:T(8,128)(2,1)}, bf16[8,512,1024]{2,1,0:T(8,128)(2,1)}) custom-call(bf16[8,128,1024]{2,1,0:T(8,128)(2,1)S(1)} %get-tuple-element.72.mine_ref, bf16[8,128,3072]{2,1,0:T(8,128)(2,1)S(1)} %get-tuple-element.83.pack_ref, bf16[8,128,3072]{2,1,0:T(8,128)(2,1)S(1)} %collective-permute-done.17.other_ref), custom_call_target="tpu_custom_call" | custom-call | flops 1048576 | bytes 1048576 | tf_op jit(solution)/shard_map/weight_pass/pallas_call | solution.py:324
  125.2 0.9 collective-permute-done.19.refs_6_
  126.1 3.8 %collective-permute-done.20.refs_7_ = bf16[96,1024]{1,0:T(8,128)(2,1)S(1)} collective-permute-done((bf16[96,1024]{1,0:T(8,128)(2,1)S(1)}, bf16[96,1024]{1,0:T(8,128)(2,1)S(1)}, u32[]{:S(2)}, u32[]{:S(2)}) %collective-permute-start.20) | collective-permute-done | bytes 196640 | tf_op jit(solution)/shard_map/ppermute | solution.py:451
  129.9 0.9 near_sum.1
  130.8 4.1 %collective-permute-done.21.back_ref = bf16[272,1024]{1,0:T(8,128)(2,1)S(1)} collective-permute-done((bf16[272,1024]{1,0:T(8,128)(2,1)S(1)}, bf16[272,1024]{1,0:T(8,128)(2,1)S(1)}, u32[]{:S(2)}, u32[]{:S(2)}) %collective-permute-start.21) | collective-permute-done | bytes 557088 | tf_op jit(solution)/shard_map/ppermute | solution.py:451
  134.9 1.3 last_sum.1
  (12 shorter events, 0.0 us)
Async XLA Ops:
  1.9 53.0 %collective-permute-start.3 = (bf16[272,1024]{1,0:T(8,128)(2,1)S(1)}, bf16[272,1024]{1,0:T(8,128)(2,1)S(1)}, u32[]{:S(2)}, u32[]{:S(2)}) collective-permute-start(bf16[272,1024]{1,0:T(8,128)(2,1)S(1)} %get-tuple-element.52.g_ref), channel_id=1, source_target_pairs={{0,8},{2,10},{4,12},{6,14},{8,0},{10,2},{12,4},{14,6},{1,9},{3,11}... | collective-permute-start | bytes 1671176 | tf_op jit(solution)/shard_map/ppermute | solution.py:451
  7.0 34.5 %collective-permute-start = (bf16[256,1024]{1,0:T(8,128)(2,1)S(1)}, bf16[256,1024]{1,0:T(8,128)(2,1)S(1)}, u32[]{:S(2)}, u32[]{:S(2)}) collective-permute-start(bf16[256,1024]{1,0:T(8,128)(2,1)S(1)} %get-tuple-element.56), channel_id=1, source_target_pairs={{0,2},{2,0},{4,6},{6,4},{8,10},{10,8},{12,14},{14,12},{1,3},{3,1},... | collective-permute-start | bytes 1572872 | tf_op jit(solution)/shard_map/ppermute | solution.py:451
  8.6 36.9 %collective-permute-start.1 = (bf16[256,1024]{1,0:T(8,128)(2,1)S(1)}, bf16[256,1024]{1,0:T(8,128)(2,1)S(1)}, u32[]{:S(2)}, u32[]{:S(2)}) collective-permute-start(bf16[256,1024]{1,0:T(8,128)(2,1)S(1)} %get-tuple-element.57), channel_id=1, source_target_pairs={{0,4},{2,6},{4,0},{6,2},{8,12},{10,14},{12,8},{14,10},{1,5},{3,7},... | collective-permute-start | bytes 1572872 | tf_op jit(solution)/shard_map/ppermute | solution.py:451
  10.2 44.8 %collective-permute-start.2 = (bf16[256,1024]{1,0:T(8,128)(2,1)S(1)}, bf16[256,1024]{1,0:T(8,128)(2,1)S(1)}, u32[]{:S(2)}, u32[]{:S(2)}) collective-permute-start(bf16[256,1024]{1,0:T(8,128)(2,1)S(1)} %get-tuple-element.58), channel_id=1, source_target_pairs={{0,6},{2,4},{4,2},{6,0},{8,14},{10,12},{12,10},{14,8},{1,7},{3,5},... | collective-permute-start | bytes 1572872 | tf_op jit(solution)/shard_map/ppermute | solution.py:451
  10.6 44.4 %collective-permute-start.4 = (bf16[256,1024]{1,0:T(8,128)(2,1)}, bf16[256,1024]{1,0:T(8,128)(2,1)S(1)}, u32[]{:S(2)}, u32[]{:S(2)}) collective-permute-start(bf16[256,1024]{1,0:T(8,128)(2,1)} %x_hbm.1), channel_id=1, source_target_pairs={{0,8},{2,10},{4,12},{6,14},{8,0},{10,2},{12,4},{14,6},{1,9},{3,11}... | collective-permute-start | bytes 1572872 | tf_op jit(solution)/shard_map/ppermute | solution.py:451
  56.7 7.7 %collective-permute-start.5 = (bf16[96,1024]{1,0:T(8,128)(2,1)S(1)}, bf16[96,1024]{1,0:T(8,128)(2,1)S(1)}, u32[]{:S(2)}, u32[]{:S(2)}) collective-permute-start(bf16[96,1024]{1,0:T(8,128)(2,1)S(1)} %get-tuple-element.60), channel_id=1, source_target_pairs={{0,2},{2,0},{4,6},{6,4},{8,10},{10,8},{12,14},{14,12},{1,3},{3,1},... | collective-permute-start | bytes 589832 | tf_op jit(solution)/shard_map/ppermute | solution.py:451
  58.2 12.3 %collective-permute-start.9 = (bf16[96,1024]{1,0:T(8,128)(2,1)}, bf16[96,1024]{1,0:T(8,128)(2,1)}, u32[]{:S(2)}, u32[]{:S(2)}) collective-permute-start(bf16[96,1024]{1,0:T(8,128)(2,1)} %get-tuple-element.67), channel_id=1, source_target_pairs={{0,4},{2,6},{4,0},{6,2},{8,12},{10,14},{12,8},{14,10},{1,5},{3,7},... | collective-permute-start | bytes 589832 | tf_op jit(solution)/shard_map/ppermute | solution.py:451
  58.2 12.3 %collective-permute-start.10 = (bf16[96,1024]{1,0:T(8,128)(2,1)}, bf16[96,1024]{1,0:T(8,128)(2,1)}, u32[]{:S(2)}, u32[]{:S(2)}) collective-permute-start(bf16[96,1024]{1,0:T(8,128)(2,1)} %get-tuple-element.68), channel_id=1, source_target_pairs={{0,6},{2,4},{4,2},{6,0},{8,14},{10,12},{12,10},{14,8},{1,7},{3,5},... | collective-permute-start | bytes 589832 | tf_op jit(solution)/shard_map/ppermute | solution.py:451
  64.4 0.7 copy-start
  67.0 14.4 %collective-permute-start.6 = (bf16[160,1024]{1,0:T(8,128)(2,1)}, bf16[160,1024]{1,0:T(8,128)(2,1)S(1)}, u32[]{:S(2)}, u32[]{:S(2)}) collective-permute-start(bf16[160,1024]{1,0:T(8,128)(2,1)} %get-tuple-element.63), channel_id=1, source_target_pairs={{0,2},{2,0},{4,6},{6,4},{8,10},{10,8},{12,14},{14,12},{1,3},{3,1},... | collective-permute-start | bytes 983048 | tf_op jit(solution)/shard_map/ppermute | solution.py:451
  68.4 15.0 %collective-permute-start.7 = (bf16[160,1024]{1,0:T(8,128)(2,1)}, bf16[160,1024]{1,0:T(8,128)(2,1)S(1)}, u32[]{:S(2)}, u32[]{:S(2)}) collective-permute-start(bf16[160,1024]{1,0:T(8,128)(2,1)} %get-tuple-element.64), channel_id=1, source_target_pairs={{0,4},{2,6},{4,0},{6,2},{8,12},{10,14},{12,8},{14,10},{1,5},{3,7},... | collective-permute-start | bytes 983048 | tf_op jit(solution)/shard_map/ppermute | solution.py:451
  68.4 16.7 %collective-permute-start.8 = (bf16[160,1024]{1,0:T(8,128)(2,1)}, bf16[160,1024]{1,0:T(8,128)(2,1)}, u32[]{:S(2)}, u32[]{:S(2)}) collective-permute-start(bf16[160,1024]{1,0:T(8,128)(2,1)} %get-tuple-element.65), channel_id=1, source_target_pairs={{0,6},{2,4},{4,2},{6,0},{8,14},{10,12},{12,10},{14,8},{1,7},{3,5},... | collective-permute-start | bytes 983048 | tf_op jit(solution)/shard_map/ppermute | solution.py:451
  70.5 0.9 copy-start.1
  79.8 18.6 %collective-permute-start.11 = (bf16[96,1024]{1,0:T(8,128)(2,1)S(1)}, bf16[96,1024]{1,0:T(8,128)(2,1)S(1)}, u32[]{:S(2)}, u32[]{:S(2)}) collective-permute-start(bf16[96,1024]{1,0:T(8,128)(2,1)S(1)} %get-tuple-element.76), channel_id=1, source_target_pairs={{0,2},{2,0},{4,6},{6,4},{8,10},{10,8},{12,14},{14,12},{1,3},{3,1},... | collective-permute-start | bytes 589832 | tf_op jit(solution)/shard_map/ppermute | solution.py:451
  81.4 19.1 %collective-permute-start.12 = (bf16[96,1024]{1,0:T(8,128)(2,1)S(1)}, bf16[96,1024]{1,0:T(8,128)(2,1)S(1)}, u32[]{:S(2)}, u32[]{:S(2)}) collective-permute-start(bf16[96,1024]{1,0:T(8,128)(2,1)S(1)} %get-tuple-element.77), channel_id=1, source_target_pairs={{0,4},{2,6},{4,0},{6,2},{8,12},{10,14},{12,8},{14,10},{1,5},{3,7},... | collective-permute-start | bytes 589832 | tf_op jit(solution)/shard_map/ppermute | solution.py:451
  81.4 19.1 %collective-permute-start.13 = (bf16[96,1024]{1,0:T(8,128)(2,1)S(1)}, bf16[96,1024]{1,0:T(8,128)(2,1)S(1)}, u32[]{:S(2)}, u32[]{:S(2)}) collective-permute-start(bf16[96,1024]{1,0:T(8,128)(2,1)S(1)} %get-tuple-element.78), channel_id=1, source_target_pairs={{0,6},{2,4},{4,2},{6,0},{8,14},{10,12},{12,10},{14,8},{1,7},{3,5},... | collective-permute-start | bytes 589832 | tf_op jit(solution)/shard_map/ppermute | solution.py:451
  96.9 5.7 %collective-permute-start.14 = (bf16[96,1024]{1,0:T(8,128)(2,1)S(1)}, bf16[96,1024]{1,0:T(8,128)(2,1)S(1)}, u32[]{:S(2)}, u32[]{:S(2)}) collective-permute-start(bf16[96,1024]{1,0:T(8,128)(2,1)S(1)} %get-tuple-element.80), channel_id=1, source_target_pairs={{0,2},{2,0},{4,6},{6,4},{8,10},{10,8},{12,14},{14,12},{1,3},{3,1},... | collective-permute-start | bytes 589832 | tf_op jit(solution)/shard_map/ppermute | solution.py:451
  98.5 5.7 %collective-permute-start.15 = (bf16[96,1024]{1,0:T(8,128)(2,1)S(1)}, bf16[96,1024]{1,0:T(8,128)(2,1)S(1)}, u32[]{:S(2)}, u32[]{:S(2)}) collective-permute-start(bf16[96,1024]{1,0:T(8,128)(2,1)S(1)} %get-tuple-element.81), channel_id=1, source_target_pairs={{0,4},{2,6},{4,0},{6,2},{8,12},{10,14},{12,8},{14,10},{1,5},{3,7},... | collective-permute-start | bytes 589832 | tf_op jit(solution)/shard_map/ppermute | solution.py:451
  98.5 7.7 %collective-permute-start.16 = (bf16[96,1024]{1,0:T(8,128)(2,1)S(1)}, bf16[96,1024]{1,0:T(8,128)(2,1)S(1)}, u32[]{:S(2)}, u32[]{:S(2)}) collective-permute-start(bf16[96,1024]{1,0:T(8,128)(2,1)S(1)} %get-tuple-element.82), channel_id=1, source_target_pairs={{0,6},{2,4},{4,2},{6,0},{8,14},{10,12},{12,10},{14,8},{1,7},{3,5},... | collective-permute-start | bytes 589832 | tf_op jit(solution)/shard_map/ppermute | solution.py:451
  107.0 10.2 %collective-permute-start.17 = (bf16[8,128,3072]{2,1,0:T(8,128)(2,1)S(1)}, bf16[8,128,3072]{2,1,0:T(8,128)(2,1)S(1)}, u32[]{:S(2)}, u32[]{:S(2)}) collective-permute-start(bf16[8,128,3072]{2,1,0:T(8,128)(2,1)S(1)} %get-tuple-element.83.pack_ref), channel_id=1, source_target_pairs={{0,1},{1,0},{2,3},{3,2},{4,5},{5,4},{6,7},{7,6},{8,9},{9,8},{10,11... | collective-permute-start | bytes 18874376 | tf_op jit(solution)/shard_map/ppermute | solution.py:454
  107.0 27.9 %collective-permute-start.21 = (bf16[272,1024]{1,0:T(8,128)(2,1)S(1)}, bf16[272,1024]{1,0:T(8,128)(2,1)S(1)}, u32[]{:S(2)}, u32[]{:S(2)}) collective-permute-start(bf16[272,1024]{1,0:T(8,128)(2,1)S(1)} %relay_sum.1), channel_id=1, source_target_pairs={{0,8},{2,10},{4,12},{6,14},{8,0},{10,2},{12,4},{14,6},{1,9},{3,11}... | collective-permute-start | bytes 1671176 | tf_op jit(solution)/shard_map/ppermute | solution.py:451
  108.9 16.3 %collective-permute-start.18 = (bf16[96,1024]{1,0:T(8,128)(2,1)S(1)}, bf16[96,1024]{1,0:T(8,128)(2,1)S(1)}, u32[]{:S(2)}, u32[]{:S(2)}) collective-permute-start(bf16[96,1024]{1,0:T(8,128)(2,1)S(1)} %get-tuple-element.91), channel_id=1, source_target_pairs={{0,2},{2,0},{4,6},{6,4},{8,10},{10,8},{12,14},{14,12},{1,3},{3,1},... | collective-permute-start | bytes 589832 | tf_op jit(solution)/shard_map/ppermute | solution.py:451
  109.7 16.5 %collective-permute-start.19 = (bf16[96,1024]{1,0:T(8,128)(2,1)S(1)}, bf16[96,1024]{1,0:T(8,128)(2,1)S(1)}, u32[]{:S(2)}, u32[]{:S(2)}) collective-permute-start(bf16[96,1024]{1,0:T(8,128)(2,1)S(1)} %get-tuple-element.92), channel_id=1, source_target_pairs={{0,4},{2,6},{4,0},{6,2},{8,12},{10,14},{12,8},{14,10},{1,5},{3,7},... | collective-permute-start | bytes 589832 | tf_op jit(solution)/shard_map/ppermute | solution.py:451
  111.6 18.3 %collective-permute-start.20 = (bf16[96,1024]{1,0:T(8,128)(2,1)S(1)}, bf16[96,1024]{1,0:T(8,128)(2,1)S(1)}, u32[]{:S(2)}, u32[]{:S(2)}) collective-permute-start(bf16[96,1024]{1,0:T(8,128)(2,1)S(1)} %get-tuple-element.93), channel_id=1, source_target_pairs={{0,6},{2,4},{4,2},{6,0},{8,14},{10,12},{12,10},{14,8},{1,7},{3,5},... | collective-permute-start | bytes 589832 | tf_op jit(solution)/shard_map/ppermute | solution.py:451
